TPU v7x, 32 devices: a whole 2x2x4 slice. The times are simulated.
32 devices in a mesh: slab: 4 (over z), brick: 8 (over y, x, core).
Axes of the slice: x: 2, y: 2, z: 4, core: 2. Of those that a mesh axis runs over, the one named last changes fastest.
Arguments:
- pressure: float32 [32, 64, 256], P('slab', 'brick'), may hold values from -6 to 6
- previous: float32 [32, 64, 256], P('slab', 'brick'), may hold values from -6 to 6
- radius: float32 [2048, 128], P(('slab', 'brick')), may hold values from 0.8 to 1.25
- velocity: float32 [2048, 128], P(('slab', 'brick')), may hold values from -1 to 1
- positions: float32 [3, 2048, 128], P(None, ('slab', 'brick')), may hold values from 0 to 1
- occupancy: int32 [2048], P(('slab', 'brick')), may hold values from 1 to 128
- anchors: int32 [3, 3, 2048], P(None, None, ('slab', 'brick')), may hold values from 0 to 224, as said below
- migrations: int32 [3, 2048], P(None, ('slab', 'brick')), may hold values from 0 to 63, as said below
- crossings: int32 [3, 32], P(None, ('slab', 'brick')), may hold values from 0 to 32, as said below
Outputs:
- final_pressure: float32 [32, 64, 256], P('slab', 'brick')
- final_radius: float32 [2048, 128], P(('slab', 'brick'))
- final_velocity: float32 [2048, 128], P(('slab', 'brick'))
Inputs may be any that keep to these rules, and one draw needn't show every extreme that they name: anchors[s, 0] lies in 0 to 7, anchors[s, 1] in 0 to 7, anchors[s, 2] in 0 to 224. `migrations`: for each step and owner the 64 listed slots are distinct local slots. `crossings`: the entry of the last brick of each slab is 0; in every step some border carries exactly 32 bins.
All inputs are finite; a program needn't handle non-finite values.
Results may differ from a plain program's by a relative error of at most 0.0003.
Values sent between devices are 32-bit elements; how exact they have to be, the bound alone decides.
A program may use at most 64 MiB of HBM per device.

v0:
```python
import jax
import jax.numpy as jnp
from jax import lax
from jax.sharding import PartitionSpec as P

BIN = 128
PZ = 32
STEPS = 3


courant_square = 0.25
source_gain = 0.05
kernel_width = 2.25
gas_pressure = 1.2
surface_tension = 0.1
viscosity = 0.02
polytropic = 1.4
sound_speed = 20.0
drive_gain = 0.5
time_step = 0.05
four_pi = 12.566370614359172


def passed_along(value, axis, steps):
    count = lax.axis_size(axis)
    leading, last = (max(0, -steps), min(count, count - steps))
    return lax.ppermute(value, axis, [(source, source + steps) for source in range(leading, last)])


def extended_2(block, sides, width):
    for axis, dim in sides:
        count = lax.axis_size(axis)
        forward = [(i, i + 1) for i in range(count - 1)]
        backward = [(target, source) for source, target in forward]
        low = lax.ppermute(
            lax.slice_in_dim(block, block.shape[dim] - width, None, axis=dim), axis, forward
        )
        high = lax.ppermute(lax.slice_in_dim(block, 0, width, axis=dim), axis, backward)
        block = jnp.concatenate([low, block, high], axis=dim)
    return block


def lead_factor(coordinate, extent, stretch):
    places = jnp.arange(extent).astype(jnp.float32)[None, :, None]
    weight = jnp.exp(-((coordinate[:, None, :] * stretch - places) ** 2) / (2.0 * kernel_width))
    return weight / jnp.sum(weight, axis=1, keepdims=True)


def wall_accel(radius, velocity, outside):
    gas_term = gas_pressure * jnp.exp(-3.0 * polytropic * jnp.log(radius))
    wall_term = gas_term - 2.0 * surface_tension / radius - 4.0 * viscosity * velocity / radius
    ambient = 1.0 + drive_gain * outside
    mach_number = velocity / sound_speed
    driving = (1.0 + mach_number) * (wall_term - ambient) - 1.5 * (
        1.0 - mach_number / 3.0
    ) * velocity * velocity
    return driving / ((1.0 - mach_number) * radius)


def bubble_block(bubbles, patches, live_count):
    slot_total = bubbles.shape[1]
    along_x = lead_factor(bubbles[2], 2, 1.0)
    along_y = lead_factor(bubbles[3], 2, 1.0)
    along_z = lead_factor(bubbles[4], PZ, PZ - 1.0)
    planar = (along_x[:, :, None, :] * along_y[:, None, :, :]).reshape(slot_total, 4, BIN)
    partial_value = jnp.einsum("gkn,gck->gcn", along_z, patches, precision=lax.Precision.HIGHEST)
    outside = jnp.sum(planar * partial_value, axis=1)
    radius, velocity = (bubbles[0], bubbles[1])
    first_accel = wall_accel(radius, velocity, outside)
    mid_radius = radius + 0.5 * time_step * velocity
    mid_velocity = velocity + 0.5 * time_step * first_accel
    second_accel = wall_accel(mid_radius, mid_velocity, outside)
    new_radius = radius + time_step * mid_velocity
    new_velocity = velocity + time_step * second_accel
    volume = four_pi * (
        2.0 * mid_radius * mid_velocity * mid_velocity + mid_radius * mid_radius * second_accel
    )
    living = jnp.arange(BIN).astype(jnp.float32)[None, :] < live_count[:, None]
    volume = jnp.where(living, volume, jnp.zeros_like(volume))
    deposit = jnp.einsum(
        "gcn,gkn->gck", planar * volume[:, None, :], along_z, precision=lax.Precision.HIGHEST
    )
    return (new_radius, new_velocity, deposit)


def read_patches(padded, corner_x, corner_y, corner_z):
    wide_y = padded.shape[1]
    depth = padded.shape[2]
    corner_index = jnp.arange(4)
    rows = (
        (corner_x[:, None] + 1 + corner_index[None, :] // 2) * wide_y
        + corner_y[:, None]
        + 1
        + corner_index[None, :] % 2
    )
    flat_index = rows[:, :, None] * depth + corner_z[:, None, None] + jnp.arange(PZ)[None, None, :]
    return jnp.take(padded.reshape(-1), flat_index)


def collect_deposit(deposit, corner_x, corner_y, corner_z, cells_x, cells_y, depth):
    slot_total = deposit.shape[0]
    depth_index = jnp.arange(depth)[None, None, :]
    window = (depth_index == corner_z[:, None, None] + jnp.arange(PZ)[None, :, None]).astype(
        jnp.float32
    )
    placed = jnp.einsum("gck,gkz->gcz", deposit, window, precision=lax.Precision.HIGHEST)
    corner_index = jnp.arange(4)
    cells = (
        (corner_x[:, None] + corner_index[None, :] // 2) * (cells_y + 1)
        + corner_y[:, None]
        + corner_index[None, :] % 2
    )
    selector = (
        cells.reshape(slot_total * 4, 1) == jnp.arange((cells_x + 1) * (cells_y + 1))[None, :]
    ).astype(jnp.float32)
    summed = jnp.einsum(
        "rm,rz->mz",
        selector,
        placed.reshape(slot_total * 4, depth),
        precision=lax.Precision.HIGHEST,
    )
    return summed.reshape(cells_x + 1, cells_y + 1, depth)


def advance(pressure, previous, padded, source):
    neighbours = padded[2:, 1:-1] + padded[:-2, 1:-1] + padded[1:-1, 2:] + padded[1:-1, :-2]
    depth_padded = jnp.pad(pressure, ((0, 0), (0, 0), (1, 1)))
    neighbours = neighbours + depth_padded[:, :, 2:] + depth_padded[:, :, :-2]
    laplace = neighbours - 6.0 * pressure
    return 2.0 * pressure - previous + courant_square * laplace + source_gain * source


def migrate(bubbles, live_count, slot_row, crossing):
    slot_total = bubbles.shape[1]
    most_count = slot_row.shape[0] // 2
    left_slots = slot_row[:most_count]
    right_slots = slot_row[most_count:]
    going_left = (bubbles[:, left_slots], live_count[left_slots])
    going_right = (bubbles[:, right_slots], live_count[right_slots], crossing)
    from_below = passed_along((going_right[0], going_right[1], going_right[2]), "brick", 1)
    from_above = passed_along((going_left[0], going_left[1]), "brick", -1)
    listed = jnp.arange(most_count)
    listed_float = listed.astype(jnp.float32)
    root = jnp.arange(slot_total)
    root = root.at[right_slots].set(
        jnp.where(listed_float < crossing, slot_total + listed, right_slots)
    )
    root = root.at[left_slots].set(
        jnp.where(listed_float < from_below[2], slot_total + most_count + listed, left_slots)
    )
    extended = jnp.concatenate([bubbles, from_above[0], from_below[0]], axis=1)
    counts_extended = jnp.concatenate([live_count, from_above[1], from_below[1]], axis=0)
    return (jnp.take(extended, root, axis=1), jnp.take(counts_extended, root, axis=0))


def local(
    pressure, previous, radius, velocity, positions, occupancy, anchors, migrations, crossings
):
    cells_x = pressure.shape[0]
    cells_y = pressure.shape[1]
    depth = pressure.shape[2]
    bubbles = jnp.concatenate([radius[None], velocity[None], positions], axis=0)
    live_count = occupancy.astype(jnp.float32)
    for step_index in range(STEPS):
        bubbles, live_count = migrate(
            bubbles, live_count, migrations[step_index], crossings[step_index].astype(jnp.float32)
        )
        padded = extended_2(pressure, (("slab", 0), ("brick", 1)), 1)
        corner_x = anchors[step_index, 0]
        corner_y = anchors[step_index, 1]
        corner_z = anchors[step_index, 2]
        patches = read_patches(padded, corner_x, corner_y, corner_z)
        new_radius, new_velocity, deposit = bubble_block(bubbles, patches, live_count)
        collected = collect_deposit(deposit, corner_x, corner_y, corner_z, cells_x, cells_y, depth)
        arrived = passed_along(collected[cells_x], "slab", 1)
        collected = collected.at[0].add(arrived)
        arrived = passed_along(collected[:cells_x, cells_y], "brick", 1)
        collected = collected.at[:cells_x, 0].add(arrived)
        source = collected[:cells_x, :cells_y]
        new_pressure = advance(pressure, previous, padded, source)
        previous, pressure = (pressure, new_pressure)
        bubbles = jnp.concatenate([new_radius[None], new_velocity[None], bubbles[2:]], axis=0)
    return (pressure, bubbles[0], bubbles[1])


def solution(mesh):
    placed = (
        P("slab", "brick", None),
        P("slab", "brick", None),
        P(("slab", "brick"), None),
        P(("slab", "brick"), None),
        P(None, ("slab", "brick"), None),
        P(("slab", "brick")),
        P(None, None, ("slab", "brick")),
        P(None, ("slab", "brick")),
        P(None, ("slab", "brick")),
    )
    return jax.shard_map(
        local,
        mesh=mesh,
        in_specs=placed,
        out_specs=(
            P("slab", "brick", None),
            P(("slab", "brick"), None),
            P(("slab", "brick"), None),
        ),
        check_vma=False,
    )
```

profile of v0, /device:TPU:12, one launch (start us, length us, event | category | flops | bytes accessed | tf_op | source)
XLA Modules:
  0.0 301.5 jit_solution(4448799837746122228)
XLA Ops:
  4.1 1.9 collective-permute-start.5
  6.6 4.5 %collective-permute-start.4 = (f32[5,32,128]{2,0,1:T(8,128)S(1)}, f32[5,32,128]{2,0,1:T(8,128)S(1)}, u32[]{:S(2)}, u32[]{:S(2)}) collective-permute-start(f32[5,32,128]{2,0,1:T(8,128)S(1)} %bitcast.327), channel_id=1, source_target_pairs={{1,0},{2,1},{3,2},{4,3},{5,4},{6,5},{7,6},{9,8},{10,9},{11,10},{12... | collective-permute-start | bytes 245768 | tf_op jit(solution)/shard_map/ppermute | solution.py:27
  12.4 2.9 collective-permute-start.28
  15.9 3.2 %collective-permute-start.6 = (f32[1]{0:T(128)}, f32[1]{0:T(128)}, u32[]{:S(2)}, u32[]{:S(2)}) collective-permute-start(f32[1]{0:T(128)} %bitcast.8), channel_id=1, source_target_pairs={{0,1},{1,2},{2,3},{3,4},{4,5},{5,6},{6,7},{8,9},{9,10},{10,11},{11... | collective-permute-start | bytes 20 | tf_op jit(solution)/shard_map/ppermute | solution.py:27
  19.8 3.0 collective-permute-start.17
  26.4 1.9 collective-permute-start.8
  28.3 4.5 %collective-permute-start.7 = (f32[32]{0:T(128)S(1)}, f32[32]{0:T(128)S(1)}, u32[]{:S(2)}, u32[]{:S(2)}) collective-permute-start(f32[32]{0:T(128)S(1)} %gather_fusion.2), channel_id=1, source_target_pairs={{1,0},{2,1},{3,2},{4,3},{5,4},{6,5},{7,6},{9,8},{10,9},{11,10},{12... | collective-permute-start | bytes 392 | tf_op jit(solution)/shard_map/ppermute | solution.py:27
  32.9 2.4 collective-permute-start
  35.2 2.0 compare_select_fusion.15
  45.6 4.5 %collective-permute-start.18 = (f32[32]{0:T(128)S(1)}, f32[32]{0:T(128)S(1)}, u32[]{:S(2)}, u32[]{:S(2)}) collective-permute-start(f32[32]{0:T(128)S(1)} %gather_fusion.6), channel_id=1, source_target_pairs={{1,0},{2,1},{3,2},{4,3},{5,4},{6,5},{7,6},{9,8},{10,9},{11,10},{12... | collective-permute-start | bytes 392 | tf_op jit(solution)/shard_map/ppermute | solution.py:27
  50.2 3.5 %collective-permute-start.1 = (f32[1,8,256]{2,0,1:T(1,128)S(1)}, f32[1,8,256]{2,0,1:T(1,128)S(1)}, u32[]{:S(2)}, u32[]{:S(2)}) collective-permute-start(f32[1,8,256]{2,0,1:T(1,128)S(1)} %copy.91), channel_id=1, source_target_pairs={{0,8},{8,16},{16,24},{1,9},{9,17},{17,25},{2,10},{10,18},{18,26},{... | collective-permute-start | bytes 24584 | tf_op jit(solution)/shard_map/ppermute | solution.py:35
  55.7 1.9 collective-permute-start.2
  57.6 2.4 collective-permute-start.3
  63.4 4.5 %collective-permute-start.29 = (f32[32]{0:T(128)S(1)}, f32[32]{0:T(128)S(1)}, u32[]{:S(2)}, u32[]{:S(2)}) collective-permute-start(f32[32]{0:T(128)S(1)} %gather_fusion.10), channel_id=1, source_target_pairs={{1,0},{2,1},{3,2},{4,3},{5,4},{6,5},{7,6},{9,8},{10,9},{11,10},{12... | collective-permute-start | bytes 392 | tf_op jit(solution)/shard_map/ppermute | solution.py:27
  68.1 45.5 %gather_fusion.14 = f32[8192]{0:T(1024)S(1)} fusion(f32[25600]{0:T(1024)S(1)} %reshape.1432, s32[8192]{0:T(1024)S(1)} %broadcast_clamp_fusion.2), kind=kCustom, calls=%fused_computation.2.clone | custom fusion | bytes 98304 | tf_op jit(solution)/shard_map/jit(_take)/gather | solution.py:97
  120.2 3.5 %collective-permute-start.9 = (f32[9,256]{1,0:T(8,128)S(1)}, f32[9,256]{1,0:T(8,128)S(1)}, u32[]{:S(2)}, u32[]{:S(2)}) collective-permute-start(f32[9,256]{1,0:T(8,128)S(1)} %slice.563), channel_id=1, source_target_pairs={{0,8},{8,16},{16,24},{1,9},{9,17},{17,25},{2,10},{10,18},{18,26},{... | collective-permute-start | bytes 27656 | tf_op jit(solution)/shard_map/ppermute | solution.py:27
  127.9 3.9 %collective-permute-done.10 = f32[8,256]{1,0:T(8,128)S(1)} collective-permute-done((f32[8,256]{1,0:T(8,128)S(1)}, f32[8,256]{1,0:T(8,128)S(1)}, u32[]{:S(2)}, u32[]{:S(2)}) %collective-permute-start.10) | collective-permute-done | bytes 8224 | tf_op jit(solution)/shard_map/ppermute | solution.py:27
  133.8 3.9 %collective-permute-start.12 = (f32[1,8,256]{2,0,1:T(1,128)S(1)}, f32[1,8,256]{2,0,1:T(1,128)S(1)}, u32[]{:S(2)}, u32[]{:S(2)}) collective-permute-start(f32[1,8,256]{2,0,1:T(1,128)S(1)} %get-tuple-element.125), channel_id=1, source_target_pairs={{0,8},{8,16},{16,24},{1,9},{9,17},{17,25},{2,10},{10,18},{18,26},{... | collective-permute-start | bytes 24584 | tf_op jit(solution)/shard_map/ppermute | solution.py:35
  139.4 1.9 collective-permute-start.13
  141.3 2.4 collective-permute-start.14
  145.1 1.9 collective-permute-start.16
  147.0 4.5 %collective-permute-start.15 = (f32[5,32,128]{2,1,0:T(8,128)S(1)}, f32[5,32,128]{2,1,0:T(8,128)S(1)}, u32[]{:S(2)}, u32[]{:S(2)}) collective-permute-start(f32[5,32,128]{2,1,0:T(8,128)S(1)} %bitcast.324), channel_id=1, source_target_pairs={{1,0},{2,1},{3,2},{4,3},{5,4},{6,5},{7,6},{9,8},{10,9},{11,10},{12... | collective-permute-start | bytes 245768 | tf_op jit(solution)/shard_map/ppermute | solution.py:27
  151.8 45.5 %gather_fusion.17 = f32[8192]{0:T(1024)S(1)} fusion(f32[25600]{0:T(1024)S(1)} %reshape.1436, s32[8192]{0:T(1024)S(1)} %broadcast_clamp_fusion.1), kind=kCustom, calls=%fused_computation.7.clone | custom fusion | bytes 98304 | tf_op jit(solution)/shard_map/jit(_take)/gather | solution.py:97
  203.9 3.9 %collective-permute-start.20 = (f32[9,256]{1,0:T(8,128)S(1)}, f32[9,256]{1,0:T(8,128)S(1)}, u32[]{:S(2)}, u32[]{:S(2)}) collective-permute-start(f32[9,256]{1,0:T(8,128)S(1)} %slice.576), channel_id=1, source_target_pairs={{0,8},{8,16},{16,24},{1,9},{9,17},{17,25},{2,10},{10,18},{18,26},{... | collective-permute-start | bytes 27656 | tf_op jit(solution)/shard_map/ppermute | solution.py:27
  209.7 1.9 collective-permute-start.21
  211.6 3.9 %collective-permute-done.21 = f32[8,256]{1,0:T(8,128)S(1)} collective-permute-done((f32[8,256]{1,0:T(8,128)S(1)}, f32[8,256]{1,0:T(8,128)S(1)}, u32[]{:S(2)}, u32[]{:S(2)}) %collective-permute-start.21) | collective-permute-done | bytes 8224 | tf_op jit(solution)/shard_map/ppermute | solution.py:27
  217.6 3.9 %collective-permute-start.23 = (f32[1,8,256]{2,0,1:T(1,128)S(1)}, f32[1,8,256]{2,0,1:T(1,128)S(1)}, u32[]{:S(2)}, u32[]{:S(2)}) collective-permute-start(f32[1,8,256]{2,0,1:T(1,128)S(1)} %get-tuple-element.123), channel_id=1, source_target_pairs={{0,8},{8,16},{16,24},{1,9},{9,17},{17,25},{2,10},{10,18},{18,26},{... | collective-permute-start | bytes 24584 | tf_op jit(solution)/shard_map/ppermute | solution.py:35
  225.1 2.4 collective-permute-start.25
  230.8 4.8 %collective-permute-start.26 = (f32[5,32,128]{2,1,0:T(8,128)S(1)}, f32[5,32,128]{2,1,0:T(8,128)S(1)}, u32[]{:S(2)}, u32[]{:S(2)}) collective-permute-start(f32[5,32,128]{2,1,0:T(8,128)S(1)} %bitcast.325), channel_id=1, source_target_pairs={{1,0},{2,1},{3,2},{4,3},{5,4},{6,5},{7,6},{9,8},{10,9},{11,10},{12... | collective-permute-start | bytes 245768 | tf_op jit(solution)/shard_map/ppermute | solution.py:27
  235.7 45.5 %gather_fusion.20 = f32[8192]{0:T(1024)S(1)} fusion(f32[25600]{0:T(1024)S(1)} %reshape.1440, s32[8192]{0:T(1024)S(1)} %broadcast_clamp_fusion), kind=kCustom, calls=%fused_computation.8.clone | custom fusion | bytes 98304 | tf_op jit(solution)/shard_map/jit(_take)/gather | solution.py:97
  289.1 3.9 %collective-permute-start.31 = (f32[9,256]{1,0:T(8,128)S(1)}, f32[9,256]{1,0:T(8,128)S(1)}, u32[]{:S(2)}, u32[]{:S(2)}) collective-permute-start(f32[9,256]{1,0:T(8,128)S(1)} %slice.589), channel_id=1, source_target_pairs={{0,8},{8,16},{16,24},{1,9},{9,17},{17,25},{2,10},{10,18},{18,26},{... | collective-permute-start | bytes 27656 | tf_op jit(solution)/shard_map/ppermute | solution.py:27
  296.8 3.9 %collective-permute-done.32 = f32[8,256]{1,0:T(8,128)S(1)} collective-permute-done((f32[8,256]{1,0:T(8,128)S(1)}, f32[8,256]{1,0:T(8,128)S(1)}, u32[]{:S(2)}, u32[]{:S(2)}) %collective-permute-start.32) | collective-permute-done | bytes 8224 | tf_op jit(solution)/shard_map/ppermute | solution.py:27
  (236 shorter events, 66.9 us)
Async XLA Ops:
  4.1 109.7 %collective-permute-start.5 = (f32[5,32,128]{2,0,1:T(8,128)S(1)}, f32[5,32,128]{2,0,1:T(8,128)S(1)}, u32[]{:S(2)}, u32[]{:S(2)}) collective-permute-start(f32[5,32,128]{2,0,1:T(8,128)S(1)} %bitcast.326), channel_id=1, source_target_pairs={{0,1},{1,2},{2,3},{3,4},{4,5},{5,6},{6,7},{8,9},{9,10},{10,11},{11... | collective-permute-start | bytes 245768 | tf_op jit(solution)/shard_map/ppermute | solution.py:27
  6.6 107.2 %collective-permute-start.4 = (f32[5,32,128]{2,0,1:T(8,128)S(1)}, f32[5,32,128]{2,0,1:T(8,128)S(1)}, u32[]{:S(2)}, u32[]{:S(2)}) collective-permute-start(f32[5,32,128]{2,0,1:T(8,128)S(1)} %bitcast.327), channel_id=1, source_target_pairs={{1,0},{2,1},{3,2},{4,3},{5,4},{6,5},{7,6},{9,8},{10,9},{11,10},{12... | collective-permute-start | bytes 245768 | tf_op jit(solution)/shard_map/ppermute | solution.py:27
  12.4 14.0 %collective-permute-start.28 = (f32[1]{0:T(128)}, f32[1]{0:T(128)}, u32[]{:S(2)}, u32[]{:S(2)}) collective-permute-start(f32[1]{0:T(128)} %bitcast.59), channel_id=1, source_target_pairs={{0,1},{1,2},{2,3},{3,4},{4,5},{5,6},{6,7},{8,9},{9,10},{10,11},{11... | collective-permute-start | bytes 20 | tf_op jit(solution)/shard_map/ppermute | solution.py:27
  15.9 12.4 %collective-permute-start.6 = (f32[1]{0:T(128)}, f32[1]{0:T(128)}, u32[]{:S(2)}, u32[]{:S(2)}) collective-permute-start(f32[1]{0:T(128)} %bitcast.8), channel_id=1, source_target_pairs={{0,1},{1,2},{2,3},{3,4},{4,5},{5,6},{6,7},{8,9},{9,10},{10,11},{11... | collective-permute-start | bytes 20 | tf_op jit(solution)/shard_map/ppermute | solution.py:27
  19.8 13.1 %collective-permute-start.17 = (f32[1]{0:T(128)}, f32[1]{0:T(128)}, u32[]{:S(2)}, u32[]{:S(2)}) collective-permute-start(f32[1]{0:T(128)} %bitcast.34), channel_id=1, source_target_pairs={{0,1},{1,2},{2,3},{3,4},{4,5},{5,6},{6,7},{8,9},{9,10},{10,11},{11... | collective-permute-start | bytes 20 | tf_op jit(solution)/shard_map/ppermute | solution.py:27
  26.4 15.0 %collective-permute-start.8 = (f32[32]{0:T(128)S(1)}, f32[32]{0:T(128)S(1)}, u32[]{:S(2)}, u32[]{:S(2)}) collective-permute-start(f32[32]{0:T(128)S(1)} %gather_fusion.3), channel_id=1, source_target_pairs={{0,1},{1,2},{2,3},{3,4},{4,5},{5,6},{6,7},{8,9},{9,10},{10,11},{11... | collective-permute-start | bytes 392 | tf_op jit(solution)/shard_map/ppermute | solution.py:27
  28.3 13.1 %collective-permute-start.7 = (f32[32]{0:T(128)S(1)}, f32[32]{0:T(128)S(1)}, u32[]{:S(2)}, u32[]{:S(2)}) collective-permute-start(f32[32]{0:T(128)S(1)} %gather_fusion.2), channel_id=1, source_target_pairs={{1,0},{2,1},{3,2},{4,3},{5,4},{6,5},{7,6},{9,8},{10,9},{11,10},{12... | collective-permute-start | bytes 392 | tf_op jit(solution)/shard_map/ppermute | solution.py:27
  32.9 21.6 %collective-permute-start = (f32[1,8,256]{2,0,1:T(1,128)S(1)}, f32[1,8,256]{2,0,1:T(1,128)S(1)}, u32[]{:S(2)}, u32[]{:S(2)}) collective-permute-start(f32[1,8,256]{2,0,1:T(1,128)S(1)} %copy.89), channel_id=1, source_target_pairs={{8,0},{16,8},{24,16},{9,1},{17,9},{25,17},{10,2},{18,10},{26,18},{... | collective-permute-start | bytes 24584 | tf_op jit(solution)/shard_map/ppermute | solution.py:38
  43.0 7.2 %collective-permute-start.19 = (f32[32]{0:T(128)S(1)}, f32[32]{0:T(128)S(1)}, u32[]{:S(2)}, u32[]{:S(2)}) collective-permute-start(f32[32]{0:T(128)S(1)} %gather_fusion.7), channel_id=1, source_target_pairs={{0,1},{1,2},{2,3},{3,4},{4,5},{5,6},{6,7},{8,9},{9,10},{10,11},{11... | collective-permute-start | bytes 392 | tf_op jit(solution)/shard_map/ppermute | solution.py:27
  45.6 8.1 %collective-permute-start.18 = (f32[32]{0:T(128)S(1)}, f32[32]{0:T(128)S(1)}, u32[]{:S(2)}, u32[]{:S(2)}) collective-permute-start(f32[32]{0:T(128)S(1)} %gather_fusion.6), channel_id=1, source_target_pairs={{1,0},{2,1},{3,2},{4,3},{5,4},{6,5},{7,6},{9,8},{10,9},{11,10},{12... | collective-permute-start | bytes 392 | tf_op jit(solution)/shard_map/ppermute | solution.py:27
  55.7 7.7 %collective-permute-start.2 = (f32[10,1,256]{2,0,1:T(8,128)S(1)}, f32[10,1,256]{2,0,1:T(8,128)S(1)}, u32[]{:S(2)}, u32[]{:S(2)}) collective-permute-start(f32[10,1,256]{2,0,1:T(8,128)S(1)} %get-tuple-element.122), channel_id=1, source_target_pairs={{1,0},{2,1},{3,2},{4,3},{5,4},{6,5},{7,6},{9,8},{10,9},{11,10},{12... | collective-permute-start | bytes 30728 | tf_op jit(solution)/shard_map/ppermute | solution.py:38
  57.6 10.3 %collective-permute-start.3 = (f32[10,1,256]{2,0,1:T(8,128)S(1)}, f32[10,1,256]{2,0,1:T(8,128)S(1)}, u32[]{:S(2)}, u32[]{:S(2)}) collective-permute-start(f32[10,1,256]{2,0,1:T(8,128)S(1)} %get-tuple-element.121), channel_id=1, source_target_pairs={{0,1},{1,2},{2,3},{3,4},{4,5},{5,6},{6,7},{8,9},{9,10},{10,11},{11... | collective-permute-start | bytes 30728 | tf_op jit(solution)/shard_map/ppermute | solution.py:35
  60.8 62.9 %collective-permute-start.30 = (f32[32]{0:T(128)S(1)}, f32[32]{0:T(128)S(1)}, u32[]{:S(2)}, u32[]{:S(2)}) collective-permute-start(f32[32]{0:T(128)S(1)} %gather_fusion.11), channel_id=1, source_target_pairs={{0,1},{1,2},{2,3},{3,4},{4,5},{5,6},{6,7},{8,9},{9,10},{10,11},{11... | collective-permute-start | bytes 392 | tf_op jit(solution)/shard_map/ppermute | solution.py:27
  63.4 60.3 %collective-permute-start.29 = (f32[32]{0:T(128)S(1)}, f32[32]{0:T(128)S(1)}, u32[]{:S(2)}, u32[]{:S(2)}) collective-permute-start(f32[32]{0:T(128)S(1)} %gather_fusion.10), channel_id=1, source_target_pairs={{1,0},{2,1},{3,2},{4,3},{5,4},{6,5},{7,6},{9,8},{10,9},{11,10},{12... | collective-permute-start | bytes 392 | tf_op jit(solution)/shard_map/ppermute | solution.py:27
  120.2 5.6 %collective-permute-start.9 = (f32[9,256]{1,0:T(8,128)S(1)}, f32[9,256]{1,0:T(8,128)S(1)}, u32[]{:S(2)}, u32[]{:S(2)}) collective-permute-start(f32[9,256]{1,0:T(8,128)S(1)} %slice.563), channel_id=1, source_target_pairs={{0,8},{8,16},{16,24},{1,9},{9,17},{17,25},{2,10},{10,18},{18,26},{... | collective-permute-start | bytes 27656 | tf_op jit(solution)/shard_map/ppermute | solution.py:27
  125.9 5.9 %collective-permute-start.10 = (f32[8,256]{1,0:T(8,128)S(1)}, f32[8,256]{1,0:T(8,128)S(1)}, u32[]{:S(2)}, u32[]{:S(2)}) collective-permute-start(f32[8,256]{1,0:T(8,128)S(1)} %slice_bitcast_fusion.10), channel_id=1, source_target_pairs={{0,1},{1,2},{2,3},{3,4},{4,5},{5,6},{6,7},{8,9},{9,10},{10,11},{11... | collective-permute-start | bytes 24584 | tf_op jit(solution)/shard_map/ppermute | solution.py:27
  131.9 5.9 %collective-permute-start.11 = (f32[1,8,256]{2,0,1:T(1,128)S(1)}, f32[1,8,256]{2,0,1:T(1,128)S(1)}, u32[]{:S(2)}, u32[]{:S(2)}) collective-permute-start(f32[1,8,256]{2,0,1:T(1,128)S(1)} %get-tuple-element.126), channel_id=1, source_target_pairs={{8,0},{16,8},{24,16},{9,1},{17,9},{25,17},{10,2},{18,10},{26,18},{... | collective-permute-start | bytes 24584 | tf_op jit(solution)/shard_map/ppermute | solution.py:38
  133.8 5.5 %collective-permute-start.12 = (f32[1,8,256]{2,0,1:T(1,128)S(1)}, f32[1,8,256]{2,0,1:T(1,128)S(1)}, u32[]{:S(2)}, u32[]{:S(2)}) collective-permute-start(f32[1,8,256]{2,0,1:T(1,128)S(1)} %get-tuple-element.125), channel_id=1, source_target_pairs={{0,8},{8,16},{16,24},{1,9},{9,17},{17,25},{2,10},{10,18},{18,26},{... | collective-permute-start | bytes 24584 | tf_op jit(solution)/shard_map/ppermute | solution.py:35
  139.4 12.2 %collective-permute-start.13 = (f32[10,1,256]{2,0,1:T(8,128)S(1)}, f32[10,1,256]{2,0,1:T(8,128)S(1)}, u32[]{:S(2)}, u32[]{:S(2)}) collective-permute-start(f32[10,1,256]{2,0,1:T(8,128)S(1)} %get-tuple-element.120), channel_id=1, source_target_pairs={{1,0},{2,1},{3,2},{4,3},{5,4},{6,5},{7,6},{9,8},{10,9},{11,10},{12... | collective-permute-start | bytes 30728 | tf_op jit(solution)/shard_map/ppermute | solution.py:38
  141.3 10.3 %collective-permute-start.14 = (f32[10,1,256]{2,0,1:T(8,128)S(1)}, f32[10,1,256]{2,0,1:T(8,128)S(1)}, u32[]{:S(2)}, u32[]{:S(2)}) collective-permute-start(f32[10,1,256]{2,0,1:T(8,128)S(1)} %get-tuple-element.119), channel_id=1, source_target_pairs={{0,1},{1,2},{2,3},{3,4},{4,5},{5,6},{6,7},{8,9},{9,10},{10,11},{11... | collective-permute-start | bytes 30728 | tf_op jit(solution)/shard_map/ppermute | solution.py:35
  145.1 52.3 %collective-permute-start.16 = (f32[5,32,128]{2,1,0:T(8,128)S(1)}, f32[5,32,128]{2,1,0:T(8,128)S(1)}, u32[]{:S(2)}, u32[]{:S(2)}) collective-permute-start(f32[5,32,128]{2,1,0:T(8,128)S(1)} %bitcast.322), channel_id=1, source_target_pairs={{0,1},{1,2},{2,3},{3,4},{4,5},{5,6},{6,7},{8,9},{9,10},{10,11},{11... | collective-permute-start | bytes 245768 | tf_op jit(solution)/shard_map/ppermute | solution.py:27
  147.0 50.4 %collective-permute-start.15 = (f32[5,32,128]{2,1,0:T(8,128)S(1)}, f32[5,32,128]{2,1,0:T(8,128)S(1)}, u32[]{:S(2)}, u32[]{:S(2)}) collective-permute-start(f32[5,32,128]{2,1,0:T(8,128)S(1)} %bitcast.324), channel_id=1, source_target_pairs={{1,0},{2,1},{3,2},{4,3},{5,4},{6,5},{7,6},{9,8},{10,9},{11,10},{12... | collective-permute-start | bytes 245768 | tf_op jit(solution)/shard_map/ppermute | solution.py:27
  203.9 5.6 %collective-permute-start.20 = (f32[9,256]{1,0:T(8,128)S(1)}, f32[9,256]{1,0:T(8,128)S(1)}, u32[]{:S(2)}, u32[]{:S(2)}) collective-permute-start(f32[9,256]{1,0:T(8,128)S(1)} %slice.576), channel_id=1, source_target_pairs={{0,8},{8,16},{16,24},{1,9},{9,17},{17,25},{2,10},{10,18},{18,26},{... | collective-permute-start | bytes 27656 | tf_op jit(solution)/shard_map/ppermute | solution.py:27
  209.7 5.9 %collective-permute-start.21 = (f32[8,256]{1,0:T(8,128)S(1)}, f32[8,256]{1,0:T(8,128)S(1)}, u32[]{:S(2)}, u32[]{:S(2)}) collective-permute-start(f32[8,256]{1,0:T(8,128)S(1)} %slice_bitcast_fusion.9), channel_id=1, source_target_pairs={{0,1},{1,2},{2,3},{3,4},{4,5},{5,6},{6,7},{8,9},{9,10},{10,11},{11... | collective-permute-start | bytes 24584 | tf_op jit(solution)/shard_map/ppermute | solution.py:27
  215.7 5.9 %collective-permute-start.22 = (f32[1,8,256]{2,0,1:T(1,128)S(1)}, f32[1,8,256]{2,0,1:T(1,128)S(1)}, u32[]{:S(2)}, u32[]{:S(2)}) collective-permute-start(f32[1,8,256]{2,0,1:T(1,128)S(1)} %get-tuple-element.124), channel_id=1, source_target_pairs={{8,0},{16,8},{24,16},{9,1},{17,9},{25,17},{10,2},{18,10},{26,18},{... | collective-permute-start | bytes 24584 | tf_op jit(solution)/shard_map/ppermute | solution.py:38
  217.6 5.5 %collective-permute-start.23 = (f32[1,8,256]{2,0,1:T(1,128)S(1)}, f32[1,8,256]{2,0,1:T(1,128)S(1)}, u32[]{:S(2)}, u32[]{:S(2)}) collective-permute-start(f32[1,8,256]{2,0,1:T(1,128)S(1)} %get-tuple-element.123), channel_id=1, source_target_pairs={{0,8},{8,16},{16,24},{1,9},{9,17},{17,25},{2,10},{10,18},{18,26},{... | collective-permute-start | bytes 24584 | tf_op jit(solution)/shard_map/ppermute | solution.py:35
  223.1 12.4 %collective-permute-start.24 = (f32[10,1,256]{2,0,1:T(8,128)S(1)}, f32[10,1,256]{2,0,1:T(8,128)S(1)}, u32[]{:S(2)}, u32[]{:S(2)}) collective-permute-start(f32[10,1,256]{2,0,1:T(8,128)S(1)} %get-tuple-element.118), channel_id=1, source_target_pairs={{1,0},{2,1},{3,2},{4,3},{5,4},{6,5},{7,6},{9,8},{10,9},{11,10},{12... | collective-permute-start | bytes 30728 | tf_op jit(solution)/shard_map/ppermute | solution.py:38
  225.1 10.5 %collective-permute-start.25 = (f32[10,1,256]{2,0,1:T(8,128)S(1)}, f32[10,1,256]{2,0,1:T(8,128)S(1)}, u32[]{:S(2)}, u32[]{:S(2)}) collective-permute-start(f32[10,1,256]{2,0,1:T(8,128)S(1)} %get-tuple-element.117), channel_id=1, source_target_pairs={{0,1},{1,2},{2,3},{3,4},{4,5},{5,6},{6,7},{8,9},{9,10},{10,11},{11... | collective-permute-start | bytes 30728 | tf_op jit(solution)/shard_map/ppermute | solution.py:35
  228.8 52.5 %collective-permute-start.27 = (f32[5,32,128]{2,1,0:T(8,128)S(1)}, f32[5,32,128]{2,1,0:T(8,128)S(1)}, u32[]{:S(2)}, u32[]{:S(2)}) collective-permute-start(f32[5,32,128]{2,1,0:T(8,128)S(1)} %bitcast.323), channel_id=1, source_target_pairs={{0,1},{1,2},{2,3},{3,4},{4,5},{5,6},{6,7},{8,9},{9,10},{10,11},{11... | collective-permute-start | bytes 245768 | tf_op jit(solution)/shard_map/ppermute | solution.py:27
  230.8 50.6 %collective-permute-start.26 = (f32[5,32,128]{2,1,0:T(8,128)S(1)}, f32[5,32,128]{2,1,0:T(8,128)S(1)}, u32[]{:S(2)}, u32[]{:S(2)}) collective-permute-start(f32[5,32,128]{2,1,0:T(8,128)S(1)} %bitcast.325), channel_id=1, source_target_pairs={{1,0},{2,1},{3,2},{4,3},{5,4},{6,5},{7,6},{9,8},{10,9},{11,10},{12... | collective-permute-start | bytes 245768 | tf_op jit(solution)/shard_map/ppermute | solution.py:27
  289.1 5.6 %collective-permute-start.31 = (f32[9,256]{1,0:T(8,128)S(1)}, f32[9,256]{1,0:T(8,128)S(1)}, u32[]{:S(2)}, u32[]{:S(2)}) collective-permute-start(f32[9,256]{1,0:T(8,128)S(1)} %slice.589), channel_id=1, source_target_pairs={{0,8},{8,16},{16,24},{1,9},{9,17},{17,25},{2,10},{10,18},{18,26},{... | collective-permute-start | bytes 27656 | tf_op jit(solution)/shard_map/ppermute | solution.py:27
  294.8 5.9 %collective-permute-start.32 = (f32[8,256]{1,0:T(8,128)S(1)}, f32[8,256]{1,0:T(8,128)S(1)}, u32[]{:S(2)}, u32[]{:S(2)}) collective-permute-start(f32[8,256]{1,0:T(8,128)S(1)} %slice_bitcast_fusion.8), channel_id=1, source_target_pairs={{0,1},{1,2},{2,3},{3,4},{4,5},{5,6},{6,7},{8,9},{9,10},{10,11},{11... | collective-permute-start | bytes 24584 | tf_op jit(solution)/shard_map/ppermute | solution.py:27
  (9 other events, 149.8 us)
where the time goes:
time: 304 us; the launch traced here: 301 us
  local copies, waits for them, and re-layouts  158 us (52%)
  starting transfers between devices  95.6 us (31%)
  waiting for transfers between devices  20.4 us (7%)
  matrix products  13.1 us (4%)
  other arithmetic  10.1 us (3%)
  between operations  4.07 us (1%)
    gather x6, local copies, waits for them, and re-layouts, read_patches(): return jnp.take(padded.reshape(-1), flat_index)  137 us
    ppermute x21, starting transfers between devices, passed_along(): lax.ppermute(value, axis, [(source, source + steps) for source in range(l...  65.1 us
    ppermute x6, starting transfers between devices, extended_2(): lax.ppermute(lax.slice_in_dim(block, block.shape[dim] - width, None, axis...  18.5 us
    ppermute x21, waiting for transfers between devices, passed_along(): lax.ppermute(value, axis, [(source, source + steps) for source in range(l...  16.2 us
    ppermute x6, starting transfers between devices, extended_2(): lax.ppermute(lax.slice_in_dim(block, 0, width, axis=dim), axis, backward)  12 us
  transfers between devices with their start and end apart: 33, of which 9 were waited for; matrix products, arithmetic and copies ran while one was open for 54% of the time, Pallas kernels for 0%

commit v1 on v0

v1 whole, which is shorter than its diff:
```python
import functools

import jax
import jax.numpy as jnp
from jax import lax
from jax.experimental import pallas as pl
from jax.experimental.pallas import tpu as pltpu
from jax.sharding import PartitionSpec as P

BIN = 128
PZ = 32
STEPS = 3

courant_square = 0.25
source_gain = 0.05
kernel_width = 2.25
gas_pressure = 1.2
surface_tension = 0.1
viscosity = 0.02
polytropic = 1.4
sound_speed = 20.0
drive_gain = 0.5
time_step = 0.05
four_pi = 12.566370614359172
root = (1.4426950408889634 / (2.0 * kernel_width)) ** 0.5

MESH = pl.DeviceIdType.MESH
F32 = jnp.float32
BF16 = jnp.bfloat16

X_HIGH, X_LOW, Y_HIGH, Y_LOW, CORNER = range(5)
DEP_X, DEP_Y, DEP_CORNER = range(5, 8)
FIX_UP, FIX_DOWN, RV_UP, RV_DOWN, COUNT = range(8, 13)
OFFSETS = (
    (-1, 0), (1, 0), (0, -1), (0, 1), (-1, -1),
    (1, 0), (0, 1), (1, 1),
    (0, 1), (0, -1), (0, 1), (0, -1), (0, 1),
)
KINDS = len(OFFSETS)


def pieces(value, count):
    found = []
    for _ in range(count - 1):
        piece = value.astype(BF16)
        found.append(piece)
        value = value - piece.astype(F32)
    found.append(value.astype(BF16))
    return found


def picked(one_hot, value, count):
    total = None
    for piece in pieces(value, count):
        term = jnp.dot(one_hot, piece, preferred_element_type=F32)
        total = term if total is None else total + term
    return total


def wall_accel(radius, velocity, outside):
    gas_term = gas_pressure * jnp.exp(-3.0 * polytropic * jnp.log(radius))
    inverse = 1.0 / radius
    wall_term = gas_term - (2.0 * surface_tension + 4.0 * viscosity * velocity) * inverse
    ambient = 1.0 + drive_gain * outside
    mach_number = velocity * (1.0 / sound_speed)
    driving = (1.0 + mach_number) * (wall_term - ambient) - 1.5 * (
        1.0 - mach_number * (1.0 / 3.0)
    ) * velocity * velocity
    return driving / ((1.0 - mach_number) * radius)


def iota(shape, dim):
    return lax.broadcasted_iota(jnp.int32, shape, dim)


def pair_factor(fraction):
    low = jnp.exp2(-jnp.square(fraction * root))
    high = jnp.exp2(-jnp.square((fraction - 1.0) * root))
    total = 1.0 / (low + high)
    return low * total, high * total


def kernel(
    slabs, bricks,
    pressure, previous, radius, velocity, positions, occupancy, anchors, migrations, crossings,
    out_pressure, out_radius, out_velocity,
    halo, edge, dep_in, dep_out, fix_in, fix_out, fix, rv_in, rv_out, rv, counts, field,
    rows, placed, fresh, corner_z, take, put, turn, send_sem, recv_sem,
):
    cells_x, cells_y, depth = pressure.shape
    bins = radius.shape[0]
    most = bins // 2
    own = cells_x * cells_y
    slab, brick = lax.axis_index("slab"), lax.axis_index("brick")

    def inside(dx, dy):
        a, b = slab + dx, brick + dy
        return (a >= 0) & (a < slabs) & (b >= 0) & (b < bricks)

    barrier = pltpu.get_barrier_semaphore()
    near = ((1, 0), (-1, 0), (0, 1), (0, -1), (1, 1), (-1, -1))
    expected = jnp.int32(0)
    for dx, dy in near:
        expected = expected + inside(dx, dy).astype(jnp.int32)

        @pl.when(inside(dx, dy))
        def _():
            pl.semaphore_signal(
                barrier, inc=1, device_id=(slab + dx, brick + dy), device_id_type=MESH
            )

    pending = []

    def copy(kind, step, source, target):
        dx, dy = OFFSETS[kind]
        return pltpu.make_async_remote_copy(
            src_ref=source,
            dst_ref=target,
            send_sem=send_sem.at[step, kind],
            recv_sem=recv_sem.at[step, kind],
            device_id=(slab + dx, brick + dy),
            device_id_type=MESH,
        )

    def send(kind, step, source, target):
        made = copy(kind, step, source, target)
        there = inside(*OFFSETS[kind])

        @pl.when(there)
        def _():
            made.start()

        pending.append((there, made))

    def arrive(kind, step, target):
        dx, dy = OFFSETS[kind]

        @pl.when(inside(-dx, -dy))
        def _():
            copy(kind, step, target, target).wait_recv()

    eye = iota((bins, bins), 0) == iota((bins, bins), 1)

    def column(row):
        return jnp.sum(jnp.where(eye, jnp.broadcast_to(row, (bins, bins)), 0.0), axis=1, keepdims=True)

    slot_row = iota((1, bins), 1).astype(F32)
    slot_column = iota((bins, 1), 0).astype(F32)
    list_rows = [migrations[s : s + 1, :].astype(F32) for s in range(STEPS)]
    list_columns = [column(row) for row in list_rows]

    def turn_of(s):
        before = slot_row if s == 0 else list_rows[s - 1]
        after = slot_column if s == STEPS else list_columns[s]
        return (after == before).astype(F32).astype(BF16)

    def send_fix(s, value):
        fix_out[s] = value
        send(FIX_UP, s, fix_out.at[s, pl.ds(most, most)], fix_in.at[s, 0])
        send(FIX_DOWN, s, fix_out.at[s, pl.ds(0, most)], fix_in.at[s, 1])

    def send_rv(s, value):
        rv_out[s] = value
        send(RV_UP, s, rv_out.at[s, pl.ds(most, most)], rv_in.at[s, 0])
        send(RV_DOWN, s, rv_out.at[s, pl.ds(0, most)], rv_in.at[s, 1])

    def send_halo(s, block):
        edge[s, 0] = jnp.concatenate([block[x, 0:1, :] for x in range(cells_x)], axis=0)
        edge[s, 1] = jnp.concatenate(
            [block[x, cells_y - 1 : cells_y, :] for x in range(cells_x)], axis=0
        )
        send(X_HIGH, s, block.at[0], halo.at[s, X_HIGH])
        send(X_LOW, s, block.at[cells_x - 1], halo.at[s, X_LOW])
        send(Y_HIGH, s, edge.at[s, 0], halo.at[s, Y_HIGH])
        send(Y_LOW, s, edge.at[s, 1], halo.at[s, Y_LOW])
        send(CORNER, s, block.at[0], halo.at[s, CORNER])

    listed = iota((most, 1), 0)

    def merged(kind_up, kind_down, s, arrived, sent):
        arrive(kind_up, s, arrived.at[s, 0])
        arrive(kind_down, s, arrived.at[s, 1])
        width = sent.shape[2]
        from_below = jnp.broadcast_to(listed < counts[1, s : s + 1, 0:1], (most, width))
        from_above = jnp.broadcast_to(listed < counts[0, s : s + 1, 0:1], (most, width))
        return jnp.concatenate(
            [
                jnp.where(from_below, arrived[s, 0], sent[s, 0:most, :]),
                jnp.where(from_above, arrived[s, 1], sent[s, most:bins, :]),
            ],
            axis=0,
        )

    count_row = iota((8, 128), 0)
    my_counts = jnp.zeros((8, 128), jnp.int32)
    for s in range(STEPS):
        my_counts = jnp.where(count_row == s, crossings[s, 0], my_counts)
    counts[0] = my_counts

    for kind in range(5):
        dx, dy = OFFSETS[kind]

        @pl.when(jnp.logical_not(inside(-dx, -dy)))
        def _():
            for s in range(STEPS):
                halo[s, kind] = jnp.zeros((cells_y, depth), F32)

    for kind in (DEP_X, DEP_Y, DEP_CORNER):
        dx, dy = OFFSETS[kind]

        @pl.when(jnp.logical_not(inside(-dx, -dy)))
        def _():
            for s in range(STEPS):
                dep_in[s, kind - 5] = jnp.zeros((cells_y, depth), F32)

    @pl.when(brick == 0)
    def _():
        counts[1] = jnp.zeros((8, 128), jnp.int32)

    alive = jnp.broadcast_to(column(occupancy[...].astype(F32)), (bins, BIN))
    first = jnp.concatenate(
        [radius[...], velocity[...], positions[0], positions[1], positions[2], alive], axis=1
    )
    first = picked(turn_of(0), first, 3)

    pl.semaphore_wait(barrier, expected)
    counts_copy = copy(COUNT, 0, counts.at[0], counts.at[1])
    there = inside(*OFFSETS[COUNT])

    @pl.when(there)
    def _():
        counts_copy.start()

    pending.append((there, counts_copy))
    send_fix(0, first[:, 2 * BIN :])
    send_halo(0, pressure)
    send_rv(0, first[:, : 2 * BIN])

    for s in range(STEPS):
        chosen = list_columns[s] == slot_row
        corner = [
            jnp.sum(
                jnp.where(chosen, anchors[s, d : d + 1, :].astype(F32), 0.0), axis=1, keepdims=True
            )
            for d in range(3)
        ]
        corner_z[s] = jnp.broadcast_to(corner[2].astype(jnp.int32), (bins, BIN))
        turn[s + 1] = turn_of(s + 1)

        def cell_of(x, y):
            return jnp.where(y < cells_y, x * cells_y + y, own + cells_y + x)

        mine = iota((bins, 4 * bins), 1) % bins == iota((bins, 4 * bins), 0)
        x_row, y_row = [
            jnp.sum(jnp.where(mine, corner[d], 0.0), axis=0, keepdims=True).astype(jnp.int32)
            for d in range(2)
        ]
        which = iota((1, 4 * bins), 1) // bins
        cells = cell_of(x_row + which // 2, y_row + which % 2)
        put[s] = (iota((128, 4 * bins), 0) == cells).astype(F32).astype(BF16)
        x_column, y_column = corner[0].astype(jnp.int32), corner[1].astype(jnp.int32)
        cells = jnp.concatenate(
            [cell_of(x_column + c // 2, y_column + c % 2) for c in range(4)], axis=0
        )
        take[s] = (iota((4 * bins, 128), 1) == cells).astype(F32).astype(BF16)

    arrive(COUNT, 0, counts.at[1])
    fix[0] = merged(FIX_UP, FIX_DOWN, 0, fix_in, fix_out)
    send_fix(1, picked(turn[1], fix[0], 3))

    lane = iota((8, 128), 1)
    for s in range(STEPS):
        now = pressure if s == 0 else field.at[s - 1]
        before = previous if s == 0 else (pressure if s == 1 else field.at[s - 2])
        for kind in (X_HIGH, Y_HIGH, CORNER):
            arrive(kind, s, halo.at[s, kind])
        corner_row = jnp.where(iota((cells_y, depth), 0) == 0, halo[s, CORNER], 0.0)
        cells = jnp.concatenate(
            [
                now[...].reshape(own, depth),
                halo[s, X_HIGH],
                halo[s, Y_HIGH],
                corner_row,
                jnp.zeros((128 - own - 3 * cells_y, depth), F32),
            ],
            axis=0,
        )
        rows[...] = picked(take[s], cells, 2)
        rv[...] = merged(RV_UP, RV_DOWN, s, rv_in, rv_out)

        def group(index, carry):
            at = pl.ds(pl.multiple_of(index * 8, 8), 8)
            start = corner_z[s, at, :]
            z = start + lane % PZ
            high = z >= 128
            z = z % 128
            patch = None
            for c in range(4):
                those = pl.ds(pl.multiple_of(c * bins + index * 8, 8), 8)
                low_part = jnp.take_along_axis(
                    rows[those, 0:128], z, axis=1, mode="promise_in_bounds"
                )
                high_part = jnp.take_along_axis(
                    rows[those, 128:256], z, axis=1, mode="promise_in_bounds"
                )
                both = jnp.where(high, high_part, low_part)
                patch = both if c == 0 else jnp.where(lane // PZ == c, both, patch)
            x_pair = pair_factor(fix[s, at, 0:BIN])
            y_pair = pair_factor(fix[s, at, BIN : 2 * BIN])
            scaled = fix[s, at, 2 * BIN : 3 * BIN] * ((PZ - 1.0) * root)
            live = fix[s, at, 3 * BIN : 4 * BIN]
            weight = [jnp.exp2(-jnp.square(scaled - k * root)) for k in range(PZ)]
            total = weight[0]
            for k in range(1, PZ):
                total = total + weight[k]
            norm = 1.0 / total
            planar = [x_pair[c // 2] * (y_pair[c % 2] * norm) for c in range(4)]
            outside = None
            for c in range(4):
                part = None
                for k in range(PZ):
                    spot = c * PZ + k
                    term = weight[k] * patch[:, spot : spot + 1]
                    part = term if part is None else part + term
                part = part * planar[c]
                outside = part if outside is None else outside + part
            r, v = rv[at, 0:BIN], rv[at, BIN : 2 * BIN]
            first_accel = wall_accel(r, v, outside)
            mid_r = r + 0.5 * time_step * v
            mid_v = v + 0.5 * time_step * first_accel
            second_accel = wall_accel(mid_r, mid_v, outside)
            fresh[at, 0:BIN] = r + time_step * mid_v
            fresh[at, BIN : 2 * BIN] = v + time_step * second_accel
            volume = four_pi * (2.0 * mid_r * mid_v * mid_v + mid_r * mid_r * second_accel)
            volume = jnp.where(lane.astype(F32) < live, volume, 0.0)
            given = jnp.zeros((8, 128), F32)
            for c in range(4):
                share = planar[c] * volume
                for k in range(PZ):
                    amount = jnp.sum(share * weight[k], axis=1, keepdims=True)
                    given = jnp.where(lane == c * PZ + k, amount, given)
            for half in range(depth // 128):
                away = lane + 128 * half - start
                valid = (away >= 0) & (away < PZ)
                away = jnp.clip(away, 0, PZ - 1)
                for c in range(4):
                    those = pl.ds(pl.multiple_of(c * bins + index * 8, 8), 8)
                    found = jnp.take_along_axis(
                        given, away + c * PZ, axis=1, mode="promise_in_bounds"
                    )
                    placed[those, 128 * half : 128 * (half + 1)] = jnp.where(valid, found, 0.0)
            return carry

        lax.fori_loop(0, bins // 8, group, 0)

        collected = picked(put[s], placed[...], 2)
        dep_out[s] = collected[own : own + 3 * cells_y, :]
        for part, kind in enumerate((DEP_X, DEP_Y, DEP_CORNER)):
            send(kind, s, dep_out.at[s, pl.ds(part * cells_y, cells_y)], dep_in.at[s, part])
        turned = picked(turn[s + 1], fresh[...], 3)
        if s + 1 < STEPS:
            send_rv(s + 1, turned)
        else:
            out_radius[...] = turned[:, :BIN]
            out_velocity[...] = turned[:, BIN:]
        if s + 1 < STEPS:
            fix[s + 1] = merged(FIX_UP, FIX_DOWN, s + 1, fix_in, fix_out)
            if s + 2 < STEPS:
                send_fix(s + 2, picked(turn[s + 2], fix[s + 1], 3))

        for kind in (X_LOW, Y_LOW):
            arrive(kind, s, halo.at[s, kind])
        after = out_pressure if s + 1 == STEPS else field.at[s]
        y_at, z_at = iota((cells_y, depth), 0), iota((cells_y, depth), 1)
        bases = []
        for x in range(cells_x):
            here = now[x]
            around = (halo[s, X_LOW] if x == 0 else now[x - 1]) + (
                halo[s, X_HIGH] if x == cells_x - 1 else now[x + 1]
            )
            around = around + jnp.where(
                y_at == 0, halo[s, Y_LOW, x : x + 1, :], pltpu.roll(here, 1, 0)
            )
            around = around + jnp.where(
                y_at == cells_y - 1, halo[s, Y_HIGH, x : x + 1, :], pltpu.roll(here, cells_y - 1, 0)
            )
            around = around + jnp.where(z_at == 0, 0.0, pltpu.roll(here, 1, 1))
            around = around + jnp.where(z_at == depth - 1, 0.0, pltpu.roll(here, depth - 1, 1))
            bases.append(
                2.0 * here
                - before[x]
                + courant_square * (around - 6.0 * here)
                + source_gain * collected[x * cells_y : (x + 1) * cells_y, :]
            )
        for part, kind in enumerate((DEP_X, DEP_Y, DEP_CORNER)):
            arrive(kind, s, dep_in.at[s, part])
        for x in range(cells_x):
            extra = jnp.where(y_at == 0, dep_in[s, 1, x : x + 1, :], 0.0)
            if x == 0:
                extra = extra + dep_in[s, 0] + dep_in[s, 2]
            after[x] = bases[x] + source_gain * extra
        if s + 1 < STEPS:
            send_halo(s + 1, after)

    for there, made in pending:

        @pl.when(there)
        def _():
            made.wait_send()


def local(
    slabs, bricks,
    pressure, previous, radius, velocity, positions, occupancy, anchors, migrations, crossings,
):
    cells_x, cells_y, depth = pressure.shape
    bins = radius.shape[0]
    most = bins // 2
    vmem = pl.BlockSpec(memory_space=pltpu.VMEM)
    smem = pl.BlockSpec(memory_space=pltpu.SMEM)
    scratch = [
        pltpu.VMEM((STEPS, 5, cells_y, depth), F32),
        pltpu.VMEM((STEPS, 2, cells_y, depth), F32),
        pltpu.VMEM((STEPS, 3, cells_y, depth), F32),
        pltpu.VMEM((STEPS, 3 * cells_y, depth), F32),
        pltpu.VMEM((STEPS, 2, most, 4 * BIN), F32),
        pltpu.VMEM((STEPS, bins, 4 * BIN), F32),
        pltpu.VMEM((STEPS, bins, 4 * BIN), F32),
        pltpu.VMEM((STEPS, 2, most, 2 * BIN), F32),
        pltpu.VMEM((STEPS, bins, 2 * BIN), F32),
        pltpu.VMEM((bins, 2 * BIN), F32),
        pltpu.VMEM((2, 8, 128), jnp.int32),
        pltpu.VMEM((STEPS - 1, cells_x, cells_y, depth), F32),
        pltpu.VMEM((4 * bins, depth), F32),
        pltpu.VMEM((4 * bins, depth), F32),
        pltpu.VMEM((bins, 2 * BIN), F32),
        pltpu.VMEM((STEPS, bins, BIN), jnp.int32),
        pltpu.VMEM((STEPS, 4 * bins, 128), BF16),
        pltpu.VMEM((STEPS, 128, 4 * bins), BF16),
        pltpu.VMEM((STEPS + 1, bins, bins), BF16),
        pltpu.SemaphoreType.DMA((STEPS, KINDS)),
        pltpu.SemaphoreType.DMA((STEPS, KINDS)),
    ]
    return pl.pallas_call(
        functools.partial(kernel, slabs, bricks),
        out_shape=(
            jax.ShapeDtypeStruct(pressure.shape, F32),
            jax.ShapeDtypeStruct(radius.shape, F32),
            jax.ShapeDtypeStruct(velocity.shape, F32),
        ),
        in_specs=[vmem] * 8 + [smem],
        out_specs=(vmem,) * 3,
        scratch_shapes=scratch,
        compiler_params=pltpu.CompilerParams(
            collective_id=0, has_side_effects=True, vmem_limit_bytes=24 * 1024 * 1024
        ),
    )(
        pressure, previous, radius, velocity, positions, occupancy.reshape(1, bins), anchors,
        migrations, crossings,
    )


def solution(mesh):
    placed = (
        P("slab", "brick", None),
        P("slab", "brick", None),
        P(("slab", "brick"), None),
        P(("slab", "brick"), None),
        P(None, ("slab", "brick"), None),
        P(("slab", "brick")),
        P(None, None, ("slab", "brick")),
        P(None, ("slab", "brick")),
        P(None, ("slab", "brick")),
    )
    return jax.shard_map(
        functools.partial(local, mesh.shape["slab"], mesh.shape["brick"]),
        mesh=mesh,
        in_specs=placed,
        out_specs=(
            P("slab", "brick", None),
            P(("slab", "brick"), None),
            P(("slab", "brick"), None),
        ),
        check_vma=False,
    )
```

time: 304 us -> 51 us (0.17)
  local copies, waits for them, and re-layouts: 158 us -> 7.93 us
  starting transfers between devices: 95.6 us -> 0 us
  Pallas kernels: 0 us -> 41.9 us
  waiting for transfers between devices: 20.4 us -> 0 us
  matrix products: 13.1 us -> 0 us
  other arithmetic: 10.1 us -> 0 us
  between operations: 4.07 us -> 0.66 us
    gather x28 -> x0, local copies, waits for them, and re-layouts: 149 us -> none  [the longest x6 137 us: read_patches(): return jnp.take(padded.reshape(-1), flat_index)]
    ppermute x33 -> x0, starting transfers between devices: 95.6 us -> none  [the longest x21 65.1 us: passed_along(): lax.ppermute(value, axis, [(source, source + steps) for source in range(l...]
    pallas_call x0 -> x1, Pallas kernels: none -> 41.9 us  [local(): pl.pallas_call(functools.partial(kernel, slabs, bricks), out_shape=(jax.S...]
    ppermute x33 -> x0, waiting for transfers between devices: 20.4 us -> none  [the longest x21 16.2 us: passed_along(): lax.ppermute(value, axis, [(source, source + steps) for source in range(l...]
    dot_general x12 -> x0, matrix products: 13.1 us -> none  [the longest x3 5.63 us: bubble_block(): jnp.einsum('gcn,gkn->gck', planar * volume[:, None, :], along_z, precisio...]
    unnamed x19 -> x22, local copies, waits for them, and re-layouts: 1.69 us -> 7.93 us
    scatter x6 -> x0, local copies, waits for them, and re-layouts: 4.04 us -> none  [the longest x3 2.02 us: migrate(): root.at[right_slots]]
    select_n x17 -> x0, other arithmetic: 3.81 us -> none  [the longest x1 1.95 us: migrate(): jnp.where(listed_float < from_below[2], slot_total + most_count + listed,...]
  transfers between devices with their start and end apart: 33 -> 0, of which waited for: 9 -> 0; matrix products, arithmetic and copies ran while one was open for 54% -> 0% of each run, Pallas kernels for 0% -> 0%
where the time goes in v1:
time: 51 us; the launch traced here: 50.5 us
  Pallas kernels  41.9 us (82%)
  local copies, waits for them, and re-layouts  7.93 us (16%)
  between operations  0.66 us (1%)
    pallas_call x1, Pallas kernels, local(): pl.pallas_call(functools.partial(kernel, slabs, bricks), out_shape=(jax.S...  41.9 us
    unnamed x22, local copies, waits for them, and re-layouts  7.93 us

profile of v1, /device:TPU:12, one launch (start us, length us, event | category | flops | bytes accessed | tf_op | source)
XLA Modules:
  0.0 50.5 jit_solution(1159761398176008412)
XLA Ops:
  0.6 0.0 copy-start.8
  0.6 0.0 copy-start.6
  0.7 0.6 %copy-done.8 = s32[3,1]{0,1:T(1,128)S(1)} copy-done((s32[3,1]{0,1:T(1,128)S(1)}, s32[3,1]{0,1:T(1,128)}, u32[]{:S(2)}) %copy-start.8) | copy-done | bytes 36
  1.3 0.0 copy-start.7
  1.3 0.1 copy.12.crossings
  1.4 0.0 copy-done.6
  1.4 0.6 %copy-done.7 = s32[64]{0:T(128)S(1)} copy-done((s32[64]{0:T(128)S(1)}, s32[64]{0:T(128)}, u32[]{:S(2)}) %copy-start.7) | copy-done | bytes 280
  1.9 0.0 copy-start
  1.9 0.9 %copy-done = f32[3,64,128]{2,1,0:T(8,128)S(1)} copy-done((f32[3,64,128]{2,1,0:T(8,128)S(1)}, f32[3,64,128]{2,1,0:T(8,128)}, u32[]{:S(2)}) %copy-start) | copy-done | bytes 98328
  2.8 0.0 copy-start.1
  2.8 0.8 %copy-done.1 = f32[8,8,256]{2,1,0:T(8,128)S(1)} copy-done((f32[8,8,256]{2,1,0:T(8,128)S(1)}, f32[8,8,256]{2,1,0:T(8,128)}, u32[]{:S(2)}) %copy-start.1) | copy-done | bytes 65560
  3.7 0.0 copy-start.2
  3.7 0.8 %copy-done.2 = f32[8,8,256]{2,1,0:T(8,128)S(1)} copy-done((f32[8,8,256]{2,1,0:T(8,128)S(1)}, f32[8,8,256]{2,1,0:T(8,128)}, u32[]{:S(2)}) %copy-start.2) | copy-done | bytes 65560
  4.5 0.0 copy-start.3
  4.5 0.8 %copy-done.3 = f32[64,128]{1,0:T(8,128)S(1)} copy-done((f32[64,128]{1,0:T(8,128)S(1)}, f32[64,128]{1,0:T(8,128)}, u32[]{:S(2)}) %copy-start.3) | copy-done | bytes 32792
  5.3 0.0 copy-start.4
  5.3 0.8 %copy-done.4 = f32[64,128]{1,0:T(8,128)S(1)} copy-done((f32[64,128]{1,0:T(8,128)S(1)}, f32[64,128]{1,0:T(8,128)}, u32[]{:S(2)}) %copy-start.4) | copy-done | bytes 32792
  6.0 0.0 copy-start.5
  6.0 0.7 %copy-done.5 = s32[3,3,64]{2,1,0:T(4,128)S(1)} copy-done((s32[3,3,64]{2,1,0:T(4,128)S(1)}, s32[3,3,64]{2,1,0:T(4,128)}, u32[]{:S(2)}) %copy-start.5) | copy-done | bytes 2328
  6.7 41.9 %shard_map.112 = (f32[8,8,256]{2,1,0:T(8,128)S(1)}, f32[64,128]{1,0:T(8,128)S(1)}, f32[64,128]{1,0:T(8,128)S(1)}) custom-call(f32[8,8,256]{2,1,0:T(8,128)S(1)} %copy-done.1, f32[8,8,256]{2,1,0:T(8,128)S(1)} %copy-done.2, f32[64,128]{1,0:T(8,128)S(1)} %copy-done.3, f32[64,128]{1,0:T(8,128)S(1)} %copy-done.4, f32[3,64,128]{2,1,0:T(8,128)S(1)} %copy-done, ...), custom_call_target="tpu_custom_call" | custom-call | tf_op jit(solution)/shard_map/pallas_call | solution.py:444
  48.7 0.6 %copy.16 = f32[8,8,256]{2,1,0:T(8,128)} copy(f32[8,8,256]{2,1,0:T(8,128)S(1)} %get-tuple-element.6) | data formatting | bytes 131072
  49.3 0.6 %copy.17 = f32[64,128]{1,0:T(8,128)} copy(f32[64,128]{1,0:T(8,128)S(1)} %get-tuple-element.7) | data formatting | bytes 65536
  49.9 0.6 %copy.18 = f32[64,128]{1,0:T(8,128)} copy(f32[64,128]{1,0:T(8,128)S(1)} %get-tuple-element.8) | data formatting | bytes 65536
Async XLA Ops:
  0.6 0.7 %copy-start.8 = (s32[3,1]{0,1:T(1,128)S(1)}, s32[3,1]{0,1:T(1,128)}, u32[]{:S(2)}) copy-start(s32[3,1]{0,1:T(1,128)} %param.17) | copy-start | bytes 40
  0.6 0.7 %copy-start.6 = (s32[3,64]{1,0:T(4,128)S(1)}, s32[3,64]{1,0:T(4,128)}, u32[]{:S(2)}) copy-start(s32[3,64]{1,0:T(4,128)} %migrations.1) | copy-start | bytes 2308
  1.3 0.7 %copy-start.7 = (s32[64]{0:T(128)S(1)}, s32[64]{0:T(128)}, u32[]{:S(2)}) copy-start(s32[64]{0:T(128)} %param.14) | copy-start | bytes 772
  1.9 0.9 %copy-start = (f32[3,64,128]{2,1,0:T(8,128)S(1)}, f32[3,64,128]{2,1,0:T(8,128)}, u32[]{:S(2)}) copy-start(f32[3,64,128]{2,1,0:T(8,128)} %positions.1) | copy-start | bytes 294916
  2.8 0.8 %copy-start.1 = (f32[8,8,256]{2,1,0:T(8,128)S(1)}, f32[8,8,256]{2,1,0:T(8,128)}, u32[]{:S(2)}) copy-start(f32[8,8,256]{2,1,0:T(8,128)} %pressure.1) | copy-start | bytes 196612
  3.7 0.8 %copy-start.2 = (f32[8,8,256]{2,1,0:T(8,128)S(1)}, f32[8,8,256]{2,1,0:T(8,128)}, u32[]{:S(2)}) copy-start(f32[8,8,256]{2,1,0:T(8,128)} %previous.1) | copy-start | bytes 196612
  4.5 0.8 %copy-start.3 = (f32[64,128]{1,0:T(8,128)S(1)}, f32[64,128]{1,0:T(8,128)}, u32[]{:S(2)}) copy-start(f32[64,128]{1,0:T(8,128)} %radius.1) | copy-start | bytes 98308
  5.3 0.8 %copy-start.4 = (f32[64,128]{1,0:T(8,128)S(1)}, f32[64,128]{1,0:T(8,128)}, u32[]{:S(2)}) copy-start(f32[64,128]{1,0:T(8,128)} %velocity.1) | copy-start | bytes 98308
  6.0 0.7 %copy-start.5 = (s32[3,3,64]{2,1,0:T(4,128)S(1)}, s32[3,3,64]{2,1,0:T(4,128)}, u32[]{:S(2)}) copy-start(s32[3,3,64]{2,1,0:T(4,128)} %anchors.1) | copy-start | bytes 6916

commit v2 on v1

--- a/solution.py
+++ b/solution.py
@@ -82,11 +82,31 @@
 
 def kernel(
     slabs, bricks,
+    pressure_hbm, previous_hbm, radius_hbm, velocity_hbm, positions_hbm, occupancy_hbm,
+    anchors_hbm, migrations_hbm, crossings_hbm,
+    out_pressure, out_radius, out_velocity,
     pressure, previous, radius, velocity, positions, occupancy, anchors, migrations, crossings,
-    out_pressure, out_radius, out_velocity,
     halo, edge, dep_in, dep_out, fix_in, fix_out, fix, rv_in, rv_out, rv, counts, field,
-    rows, placed, fresh, corner_z, take, put, turn, send_sem, recv_sem,
+    rows, placed, fresh, corner_z, take, put, turn, parts, shares, planar, norms, w_high, w_low,
+    send_sem, recv_sem, load_sem,
 ):
+    loads = {}
+    for index, (name, source, target) in enumerate(
+        (
+            ("migrations", migrations_hbm, migrations),
+            ("radius", radius_hbm, radius),
+            ("velocity", velocity_hbm, velocity),
+            ("positions", positions_hbm, positions),
+            ("occupancy", occupancy_hbm, occupancy),
+            ("pressure", pressure_hbm, pressure),
+            ("crossings", crossings_hbm, crossings),
+            ("anchors", anchors_hbm, anchors),
+            ("previous", previous_hbm, previous),
+        )
+    ):
+        loads[name] = pltpu.make_async_copy(source, target, load_sem.at[index])
+        loads[name].start()
+
     cells_x, cells_y, depth = pressure.shape
     bins = radius.shape[0]
     most = bins // 2
@@ -139,6 +159,7 @@
         def _():
             copy(kind, step, target, target).wait_recv()
 
+    loads["migrations"].wait()
     eye = iota((bins, bins), 0) == iota((bins, bins), 1)
 
     def column(row):
@@ -192,10 +213,6 @@
         )
 
     count_row = iota((8, 128), 0)
-    my_counts = jnp.zeros((8, 128), jnp.int32)
-    for s in range(STEPS):
-        my_counts = jnp.where(count_row == s, crossings[s, 0], my_counts)
-    counts[0] = my_counts
 
     for kind in range(5):
         dx, dy = OFFSETS[kind]
@@ -217,6 +234,14 @@
     def _():
         counts[1] = jnp.zeros((8, 128), jnp.int32)
 
+    for name in ("radius", "velocity", "positions", "occupancy", "pressure", "crossings"):
+        loads[name].wait()
+    my_counts = jnp.zeros((8, 128), jnp.int32)
+    for s in range(STEPS):
+        my_counts = jnp.where(
+            count_row == s, jnp.broadcast_to(crossings[s : s + 1, :], (8, 128)), my_counts
+        )
+    counts[0] = my_counts
     alive = jnp.broadcast_to(column(occupancy[...].astype(F32)), (bins, BIN))
     first = jnp.concatenate(
         [radius[...], velocity[...], positions[0], positions[1], positions[2], alive], axis=1
@@ -236,39 +261,61 @@
     send_halo(0, pressure)
     send_rv(0, first[:, : 2 * BIN])
 
+    loads["anchors"].wait()
+    patch_rows = 4 * bins
+    owner = iota((patch_rows, bins), 0) // 4 == iota((patch_rows, bins), 1)
+    which = iota((patch_rows, 1), 0) % 4
+    square = iota((patch_rows, patch_rows), 0) == iota((patch_rows, patch_rows), 1)
     for s in range(STEPS):
-        chosen = list_columns[s] == slot_row
-        corner = [
+        turn[s + 1] = turn_of(s + 1)
+        listed_slot = jnp.sum(jnp.where(owner, list_rows[s], 0.0), axis=1, keepdims=True)
+        chosen = listed_slot == slot_row
+        x, y, z = [
             jnp.sum(
                 jnp.where(chosen, anchors[s, d : d + 1, :].astype(F32), 0.0), axis=1, keepdims=True
-            )
+            ).astype(jnp.int32)
             for d in range(3)
         ]
-        corner_z[s] = jnp.broadcast_to(corner[2].astype(jnp.int32), (bins, BIN))
-        turn[s + 1] = turn_of(s + 1)
-
-        def cell_of(x, y):
-            return jnp.where(y < cells_y, x * cells_y + y, own + cells_y + x)
-
-        mine = iota((bins, 4 * bins), 1) % bins == iota((bins, 4 * bins), 0)
-        x_row, y_row = [
-            jnp.sum(jnp.where(mine, corner[d], 0.0), axis=0, keepdims=True).astype(jnp.int32)
-            for d in range(2)
-        ]
-        which = iota((1, 4 * bins), 1) // bins
-        cells = cell_of(x_row + which // 2, y_row + which % 2)
-        put[s] = (iota((128, 4 * bins), 0) == cells).astype(F32).astype(BF16)
-        x_column, y_column = corner[0].astype(jnp.int32), corner[1].astype(jnp.int32)
-        cells = jnp.concatenate(
-            [cell_of(x_column + c // 2, y_column + c % 2) for c in range(4)], axis=0
-        )
-        take[s] = (iota((4 * bins, 128), 1) == cells).astype(F32).astype(BF16)
+        corner_z[s] = jnp.broadcast_to(z, (patch_rows, BIN))
+        x, y = x + which // 2, y + which % 2
+        cells = jnp.where(y < cells_y, x * cells_y + y, own + cells_y + x)
+        take[s] = (iota((patch_rows, 128), 1) == cells).astype(F32).astype(BF16)
+        cells = jnp.sum(jnp.where(square, cells.astype(F32), 0.0), axis=0, keepdims=True)
+        put[s] = (iota((128, patch_rows), 0).astype(F32) == cells).astype(F32).astype(BF16)
+
+    far = iota((PZ, BIN), 0).astype(F32) * root
+
+    def build_weights(s):
+        def group(index, carry):
+            at = pl.ds(pl.multiple_of(index * 8, 8), 8)
+            scaled = fix[s, at, 2 * BIN : 3 * BIN] * ((PZ - 1.0) * root)
+            totals = []
+            for g in range(8):
+                weight = jnp.exp2(-jnp.square(scaled[g : g + 1, :] - far))
+                totals.append(jnp.sum(weight, axis=0, keepdims=True))
+                those = pl.ds(pl.multiple_of(index * (8 * PZ) + g * PZ, PZ), PZ)
+                high = weight.astype(BF16)
+                w_high[those, :] = high
+                w_low[those, :] = (weight - high.astype(F32)).astype(BF16)
+            norms[at, :] = jnp.concatenate(totals, axis=0)
+            return carry
+
+        lax.fori_loop(0, bins // 8, group, 0)
+        x_pair = pair_factor(fix[s, :, 0:BIN])
+        y_pair = pair_factor(fix[s, :, BIN : 2 * BIN])
+        norm = 1.0 / norms[...]
+        for c in range(4):
+            planar[c] = x_pair[c // 2] * (y_pair[c % 2] * norm)
 
     arrive(COUNT, 0, counts.at[1])
     fix[0] = merged(FIX_UP, FIX_DOWN, 0, fix_in, fix_out)
     send_fix(1, picked(turn[1], fix[0], 3))
+    build_weights(0)
+    loads["previous"].wait()
 
     lane = iota((8, 128), 1)
+    bin_in_four = [2 * h + iota((8, 128), 0) // 4 for h in range(2)]
+    nt = (((1,), (1,)), ((), ()))
     for s in range(STEPS):
         now = pressure if s == 0 else field.at[s - 1]
         before = previous if s == 0 else (pressure if s == 1 else field.at[s - 2])
@@ -288,70 +335,65 @@
         rows[...] = picked(take[s], cells, 2)
         rv[...] = merged(RV_UP, RV_DOWN, s, rv_in, rv_out)
 
-        def group(index, carry):
-            at = pl.ds(pl.multiple_of(index * 8, 8), 8)
-            start = corner_z[s, at, :]
-            z = start + lane % PZ
-            high = z >= 128
-            z = z % 128
-            patch = None
-            for c in range(4):
-                those = pl.ds(pl.multiple_of(c * bins + index * 8, 8), 8)
-                low_part = jnp.take_along_axis(
-                    rows[those, 0:128], z, axis=1, mode="promise_in_bounds"
-                )
-                high_part = jnp.take_along_axis(
-                    rows[those, 128:256], z, axis=1, mode="promise_in_bounds"
-                )
-                both = jnp.where(high, high_part, low_part)
-                patch = both if c == 0 else jnp.where(lane // PZ == c, both, patch)
-            x_pair = pair_factor(fix[s, at, 0:BIN])
-            y_pair = pair_factor(fix[s, at, BIN : 2 * BIN])
-            scaled = fix[s, at, 2 * BIN : 3 * BIN] * ((PZ - 1.0) * root)
-            live = fix[s, at, 3 * BIN : 4 * BIN]
-            weight = [jnp.exp2(-jnp.square(scaled - k * root)) for k in range(PZ)]
-            total = weight[0]
-            for k in range(1, PZ):
-                total = total + weight[k]
-            norm = 1.0 / total
-            planar = [x_pair[c // 2] * (y_pair[c % 2] * norm) for c in range(4)]
-            outside = None
-            for c in range(4):
-                part = None
-                for k in range(PZ):
-                    spot = c * PZ + k
-                    term = weight[k] * patch[:, spot : spot + 1]
-                    part = term if part is None else part + term
-                part = part * planar[c]
-                outside = part if outside is None else outside + part
-            r, v = rv[at, 0:BIN], rv[at, BIN : 2 * BIN]
-            first_accel = wall_accel(r, v, outside)
-            mid_r = r + 0.5 * time_step * v
-            mid_v = v + 0.5 * time_step * first_accel
-            second_accel = wall_accel(mid_r, mid_v, outside)
-            fresh[at, 0:BIN] = r + time_step * mid_v
-            fresh[at, BIN : 2 * BIN] = v + time_step * second_accel
-            volume = four_pi * (2.0 * mid_r * mid_v * mid_v + mid_r * mid_r * second_accel)
-            volume = jnp.where(lane.astype(F32) < live, volume, 0.0)
-            given = jnp.zeros((8, 128), F32)
-            for c in range(4):
-                share = planar[c] * volume
-                for k in range(PZ):
-                    amount = jnp.sum(share * weight[k], axis=1, keepdims=True)
-                    given = jnp.where(lane == c * PZ + k, amount, given)
-            for half in range(depth // 128):
-                away = lane + 128 * half - start
-                valid = (away >= 0) & (away < PZ)
-                away = jnp.clip(away, 0, PZ - 1)
-                for c in range(4):
-                    those = pl.ds(pl.multiple_of(c * bins + index * 8, 8), 8)
+        for q in range(bins // 4):
+            halves = []
+            for h in range(2):
+                at = slice(16 * q + 8 * h, 16 * q + 8 * h + 8)
+                z = corner_z[s, at, :] + lane % PZ
+                found = [
+                    jnp.take_along_axis(
+                        rows[at, 128 * part : 128 * (part + 1)],
+                        z % 128,
+                        axis=1,
+                        mode="promise_in_bounds",
+                    )
+                    for part in range(depth // 128)
+                ]
+                patch = jnp.where(z >= 128, found[1], found[0])
+                halves.append(jnp.where(lane // PZ == bin_in_four[h], patch, 0.0))
+            high, low = pieces(jnp.concatenate(halves, axis=0), 2)
+            four = slice(128 * q, 128 * (q + 1))
+            parts[16 * q : 16 * (q + 1), :] = (
+                jnp.dot(high, w_high[four, :], preferred_element_type=F32)
+                + jnp.dot(low, w_high[four, :], preferred_element_type=F32)
+                + jnp.dot(high, w_low[four, :], preferred_element_type=F32)
+            )
+        outside = None
+        for c in range(4):
+            term = planar[c] * parts[pl.ds(c, bins, stride=4), :]
+            outside = term if outside is None else outside + term
+        r, v = rv[:, 0:BIN], rv[:, BIN : 2 * BIN]
+        first_accel = wall_accel(r, v, outside)
+        mid_r = r + 0.5 * time_step * v
+        mid_v = v + 0.5 * time_step * first_accel
+        second_accel = wall_accel(mid_r, mid_v, outside)
+        fresh[:, 0:BIN] = r + time_step * mid_v
+        fresh[:, BIN : 2 * BIN] = v + time_step * second_accel
+        volume = four_pi * (2.0 * mid_r * mid_v * mid_v + mid_r * mid_r * second_accel)
+        live = iota((bins, BIN), 1).astype(F32) < fix[s, :, 3 * BIN : 4 * BIN]
+        volume = jnp.where(live, volume, 0.0)
+        for c in range(4):
+            shares[pl.ds(c, bins, stride=4), :] = planar[c] * volume
+        for q in range(bins // 4):
+            high, low = pieces(shares[16 * q : 16 * (q + 1), :], 2)
+            four = slice(128 * q, 128 * (q + 1))
+            given = (
+                lax.dot_general(high, w_high[four, :], nt, preferred_element_type=F32)
+                + lax.dot_general(low, w_high[four, :], nt, preferred_element_type=F32)
+                + lax.dot_general(high, w_low[four, :], nt, preferred_element_type=F32)
+            )
+            for h in range(2):
+                at = slice(16 * q + 8 * h, 16 * q + 8 * h + 8)
+                for part in range(depth // 128):
+                    away = lane + 128 * part - corner_z[s, at, :]
+                    valid = (away >= 0) & (away < PZ)
                     found = jnp.take_along_axis(
-                        given, away + c * PZ, axis=1, mode="promise_in_bounds"
+                        given[8 * h : 8 * h + 8, :],
+                        jnp.clip(away, 0, PZ - 1) + PZ * bin_in_four[h],
+                        axis=1,
+                        mode="promise_in_bounds",
                     )
-                    placed[those, 128 * half : 128 * (half + 1)] = jnp.where(valid, found, 0.0)
-            return carry
-
-        lax.fori_loop(0, bins // 8, group, 0)
+                    placed[at, 128 * part : 128 * (part + 1)] = jnp.where(valid, found, 0.0)
 
         collected = picked(put[s], placed[...], 2)
         dep_out[s] = collected[own : own + 3 * cells_y, :]
@@ -367,6 +409,7 @@
             fix[s + 1] = merged(FIX_UP, FIX_DOWN, s + 1, fix_in, fix_out)
             if s + 2 < STEPS:
                 send_fix(s + 2, picked(turn[s + 2], fix[s + 1], 3))
+            build_weights(s + 1)
 
         for kind in (X_LOW, Y_LOW):
             arrive(kind, s, halo.at[s, kind])
@@ -417,8 +460,17 @@
     bins = radius.shape[0]
     most = bins // 2
     vmem = pl.BlockSpec(memory_space=pltpu.VMEM)
-    smem = pl.BlockSpec(memory_space=pltpu.SMEM)
+    hbm = pl.BlockSpec(memory_space=pltpu.HBM)
     scratch = [
+        pltpu.VMEM(pressure.shape, F32),
+        pltpu.VMEM(previous.shape, F32),
+        pltpu.VMEM(radius.shape, F32),
+        pltpu.VMEM(velocity.shape, F32),
+        pltpu.VMEM(positions.shape, F32),
+        pltpu.VMEM((1, bins), jnp.int32),
+        pltpu.VMEM(anchors.shape, jnp.int32),
+        pltpu.VMEM(migrations.shape, jnp.int32),
+        pltpu.VMEM(crossings.shape, jnp.int32),
         pltpu.VMEM((STEPS, 5, cells_y, depth), F32),
         pltpu.VMEM((STEPS, 2, cells_y, depth), F32),
         pltpu.VMEM((STEPS, 3, cells_y, depth), F32),
@@ -434,12 +486,19 @@
         pltpu.VMEM((4 * bins, depth), F32),
         pltpu.VMEM((4 * bins, depth), F32),
         pltpu.VMEM((bins, 2 * BIN), F32),
-        pltpu.VMEM((STEPS, bins, BIN), jnp.int32),
+        pltpu.VMEM((STEPS, 4 * bins, BIN), jnp.int32),
         pltpu.VMEM((STEPS, 4 * bins, 128), BF16),
         pltpu.VMEM((STEPS, 128, 4 * bins), BF16),
         pltpu.VMEM((STEPS + 1, bins, bins), BF16),
+        pltpu.VMEM((4 * bins, BIN), F32),
+        pltpu.VMEM((4 * bins, BIN), F32),
+        pltpu.VMEM((4, bins, BIN), F32),
+        pltpu.VMEM((bins, BIN), F32),
+        pltpu.VMEM((PZ * bins, BIN), BF16),
+        pltpu.VMEM((PZ * bins, BIN), BF16),
         pltpu.SemaphoreType.DMA((STEPS, KINDS)),
         pltpu.SemaphoreType.DMA((STEPS, KINDS)),
+        pltpu.SemaphoreType.DMA((9,)),
     ]
     return pl.pallas_call(
         functools.partial(kernel, slabs, bricks),
@@ -448,7 +507,7 @@
             jax.ShapeDtypeStruct(radius.shape, F32),
             jax.ShapeDtypeStruct(velocity.shape, F32),
         ),
-        in_specs=[vmem] * 8 + [smem],
+        in_specs=[hbm] * 9,
         out_specs=(vmem,) * 3,
         scratch_shapes=scratch,
         compiler_params=pltpu.CompilerParams(

time: 51 us -> 38.5 us (0.75)
  Pallas kernels: 41.9 us -> 29.5 us
    pallas_call x1, Pallas kernels: 41.9 us -> 29.5 us  [local(): pl.pallas_call(functools.partial(kernel, slabs, bricks), out_shape=(jax.S...]
where the time goes in v2:
time: 38.5 us; the launch traced here: 38.1 us
  Pallas kernels  29.5 us (77%)
  local copies, waits for them, and re-layouts  7.93 us (21%)
  between operations  0.66 us (2%)
    pallas_call x1, Pallas kernels, local(): pl.pallas_call(functools.partial(kernel, slabs, bricks), out_shape=(jax.S...  29.5 us
    unnamed x22, local copies, waits for them, and re-layouts  7.93 us

profile of v2, /device:TPU:12, one launch (start us, length us, event | category | flops | bytes accessed | tf_op | source)
XLA Modules:
  0.0 38.1 jit_solution(11214655874638686687)
XLA Ops:
  0.6 0.0 copy-start.8
  0.6 0.0 copy-start.6
  0.7 0.6 %copy-done.8 = s32[3,1]{0,1:T(1,128)S(1)} copy-done((s32[3,1]{0,1:T(1,128)S(1)}, s32[3,1]{0,1:T(1,128)}, u32[]{:S(2)}) %copy-start.8) | copy-done | bytes 36
  1.3 0.0 copy-start.7
  1.3 0.1 copy.12.crossings_hbm
  1.4 0.0 copy-done.6
  1.4 0.6 %copy-done.7 = s32[64]{0:T(128)S(1)} copy-done((s32[64]{0:T(128)S(1)}, s32[64]{0:T(128)}, u32[]{:S(2)}) %copy-start.7) | copy-done | bytes 280
  1.9 0.0 copy-start
  1.9 0.9 %copy-done = f32[3,64,128]{2,1,0:T(8,128)S(1)} copy-done((f32[3,64,128]{2,1,0:T(8,128)S(1)}, f32[3,64,128]{2,1,0:T(8,128)}, u32[]{:S(2)}) %copy-start) | copy-done | bytes 98328
  2.8 0.0 copy-start.1
  2.8 0.8 %copy-done.1 = f32[8,8,256]{2,1,0:T(8,128)S(1)} copy-done((f32[8,8,256]{2,1,0:T(8,128)S(1)}, f32[8,8,256]{2,1,0:T(8,128)}, u32[]{:S(2)}) %copy-start.1) | copy-done | bytes 65560
  3.7 0.0 copy-start.2
  3.7 0.8 %copy-done.2 = f32[8,8,256]{2,1,0:T(8,128)S(1)} copy-done((f32[8,8,256]{2,1,0:T(8,128)S(1)}, f32[8,8,256]{2,1,0:T(8,128)}, u32[]{:S(2)}) %copy-start.2) | copy-done | bytes 65560
  4.5 0.0 copy-start.3
  4.5 0.8 %copy-done.3 = f32[64,128]{1,0:T(8,128)S(1)} copy-done((f32[64,128]{1,0:T(8,128)S(1)}, f32[64,128]{1,0:T(8,128)}, u32[]{:S(2)}) %copy-start.3) | copy-done | bytes 32792
  5.3 0.0 copy-start.4
  5.3 0.8 %copy-done.4 = f32[64,128]{1,0:T(8,128)S(1)} copy-done((f32[64,128]{1,0:T(8,128)S(1)}, f32[64,128]{1,0:T(8,128)}, u32[]{:S(2)}) %copy-start.4) | copy-done | bytes 32792
  6.0 0.0 copy-start.5
  6.0 0.7 %copy-done.5 = s32[3,3,64]{2,1,0:T(4,128)S(1)} copy-done((s32[3,3,64]{2,1,0:T(4,128)S(1)}, s32[3,3,64]{2,1,0:T(4,128)}, u32[]{:S(2)}) %copy-start.5) | copy-done | bytes 2328
  6.7 29.5 %shard_map.112 = (f32[8,8,256]{2,1,0:T(8,128)S(1)}, f32[64,128]{1,0:T(8,128)S(1)}, f32[64,128]{1,0:T(8,128)S(1)}) custom-call(f32[8,8,256]{2,1,0:T(8,128)S(1)} %copy-done.1, f32[8,8,256]{2,1,0:T(8,128)S(1)} %copy-done.2, f32[64,128]{1,0:T(8,128)S(1)} %copy-done.3, f32[64,128]{1,0:T(8,128)S(1)} %copy-done.4, f32[3,64,128]{2,1,0:T(8,128)S(1)} %copy-done, ...), custom_call_target="tpu_custom_call" | custom-call | tf_op jit(solution)/shard_map/pallas_call | solution.py:503
  36.2 0.6 %copy.16 = f32[8,8,256]{2,1,0:T(8,128)} copy(f32[8,8,256]{2,1,0:T(8,128)S(1)} %get-tuple-element.6) | data formatting | bytes 131072
  36.8 0.6 %copy.17 = f32[64,128]{1,0:T(8,128)} copy(f32[64,128]{1,0:T(8,128)S(1)} %get-tuple-element.7) | data formatting | bytes 65536
  37.5 0.6 %copy.18 = f32[64,128]{1,0:T(8,128)} copy(f32[64,128]{1,0:T(8,128)S(1)} %get-tuple-element.8) | data formatting | bytes 65536
Async XLA Ops:
  0.6 0.7 %copy-start.8 = (s32[3,1]{0,1:T(1,128)S(1)}, s32[3,1]{0,1:T(1,128)}, u32[]{:S(2)}) copy-start(s32[3,1]{0,1:T(1,128)} %param.17) | copy-start | bytes 40
  0.6 0.7 %copy-start.6 = (s32[3,64]{1,0:T(4,128)S(1)}, s32[3,64]{1,0:T(4,128)}, u32[]{:S(2)}) copy-start(s32[3,64]{1,0:T(4,128)} %migrations_hbm.1) | copy-start | bytes 2308
  1.3 0.7 %copy-start.7 = (s32[64]{0:T(128)S(1)}, s32[64]{0:T(128)}, u32[]{:S(2)}) copy-start(s32[64]{0:T(128)} %param.14) | copy-start | bytes 772
  1.9 0.9 %copy-start = (f32[3,64,128]{2,1,0:T(8,128)S(1)}, f32[3,64,128]{2,1,0:T(8,128)}, u32[]{:S(2)}) copy-start(f32[3,64,128]{2,1,0:T(8,128)} %positions_hbm.1) | copy-start | bytes 294916
  2.8 0.8 %copy-start.1 = (f32[8,8,256]{2,1,0:T(8,128)S(1)}, f32[8,8,256]{2,1,0:T(8,128)}, u32[]{:S(2)}) copy-start(f32[8,8,256]{2,1,0:T(8,128)} %pressure_hbm.1) | copy-start | bytes 196612
  3.7 0.8 %copy-start.2 = (f32[8,8,256]{2,1,0:T(8,128)S(1)}, f32[8,8,256]{2,1,0:T(8,128)}, u32[]{:S(2)}) copy-start(f32[8,8,256]{2,1,0:T(8,128)} %previous_hbm.1) | copy-start | bytes 196612
  4.5 0.8 %copy-start.3 = (f32[64,128]{1,0:T(8,128)S(1)}, f32[64,128]{1,0:T(8,128)}, u32[]{:S(2)}) copy-start(f32[64,128]{1,0:T(8,128)} %radius_hbm.1) | copy-start | bytes 98308
  5.3 0.8 %copy-start.4 = (f32[64,128]{1,0:T(8,128)S(1)}, f32[64,128]{1,0:T(8,128)}, u32[]{:S(2)}) copy-start(f32[64,128]{1,0:T(8,128)} %velocity_hbm.1) | copy-start | bytes 98308
  6.0 0.7 %copy-start.5 = (s32[3,3,64]{2,1,0:T(4,128)S(1)}, s32[3,3,64]{2,1,0:T(4,128)}, u32[]{:S(2)}) copy-start(s32[3,3,64]{2,1,0:T(4,128)} %anchors_hbm.1) | copy-start | bytes 6916

commit v3 on v2

--- a/solution.py
+++ b/solution.py
@@ -239,7 +239,7 @@
     my_counts = jnp.zeros((8, 128), jnp.int32)
     for s in range(STEPS):
         my_counts = jnp.where(
-            count_row == s, jnp.broadcast_to(crossings[s : s + 1, :], (8, 128)), my_counts
+            count_row == s, jnp.broadcast_to(crossings[:, s : s + 1], (8, 128)), my_counts
         )
     counts[0] = my_counts
     alive = jnp.broadcast_to(column(occupancy[...].astype(F32)), (bins, BIN))
@@ -470,7 +470,7 @@
         pltpu.VMEM((1, bins), jnp.int32),
         pltpu.VMEM(anchors.shape, jnp.int32),
         pltpu.VMEM(migrations.shape, jnp.int32),
-        pltpu.VMEM(crossings.shape, jnp.int32),
+        pltpu.VMEM((1, STEPS), jnp.int32),
         pltpu.VMEM((STEPS, 5, cells_y, depth), F32),
         pltpu.VMEM((STEPS, 2, cells_y, depth), F32),
         pltpu.VMEM((STEPS, 3, cells_y, depth), F32),
@@ -500,7 +500,7 @@
         pltpu.SemaphoreType.DMA((STEPS, KINDS)),
         pltpu.SemaphoreType.DMA((9,)),
     ]
-    return pl.pallas_call(
+    results = pl.pallas_call(
         functools.partial(kernel, slabs, bricks),
         out_shape=(
             jax.ShapeDtypeStruct(pressure.shape, F32),
@@ -511,12 +511,34 @@
         out_specs=(vmem,) * 3,
         scratch_shapes=scratch,
         compiler_params=pltpu.CompilerParams(
-            collective_id=0, has_side_effects=True, vmem_limit_bytes=24 * 1024 * 1024
+            collective_id=0, has_side_effects=True, vmem_limit_bytes=60 * 1024 * 1024
         ),
     )(
         pressure, previous, radius, velocity, positions, occupancy.reshape(1, bins), anchors,
-        migrations, crossings,
+        migrations, crossings.reshape(1, STEPS),
     )
+    return pl.pallas_call(
+        handed_on,
+        out_shape=tuple(jax.ShapeDtypeStruct(x.shape, F32) for x in results),
+        in_specs=[hbm] * 3,
+        out_specs=(hbm,) * 3,
+        scratch_shapes=[pltpu.VMEM(x.shape, F32) for x in results]
+        + [pltpu.SemaphoreType.DMA((2, 3))],
+        compiler_params=pltpu.CompilerParams(vmem_limit_bytes=60 * 1024 * 1024),
+    )(*results)
+
+
+def handed_on(*refs):
+    given, wanted, held, sem = refs[:3], refs[3:6], refs[6:9], refs[9]
+    fetched = [pltpu.make_async_copy(given[i], held[i], sem.at[0, i]) for i in range(3)]
+    stored = [pltpu.make_async_copy(held[i], wanted[i], sem.at[1, i]) for i in range(3)]
+    for copy in fetched:
+        copy.start()
+    for i in range(3):
+        fetched[i].wait()
+        stored[i].start()
+    for copy in stored:
+        copy.wait()
 
 
 def solution(mesh):

time: 38.5 us -> 32.2 us (0.84)
  local copies, waits for them, and re-layouts: 7.93 us -> 0 us
  Pallas kernels: 29.5 us -> 31.3 us
    unnamed x22 -> x0, local copies, waits for them, and re-layouts: 7.93 us -> none
    pallas_call x0 -> x1, Pallas kernels: none -> 1.54 us  [local(): pl.pallas_call(handed_on, out_shape=tuple((jax.ShapeDtypeStruct(x.shape,...]
where the time goes in v3:
time: 32.2 us; the launch traced here: 32 us
  Pallas kernels  31.3 us (97%)
  between operations  0.64 us (2%)
    pallas_call x1, Pallas kernels, local(): pl.pallas_call(functools.partial(kernel, slabs, bricks), out_shape=(jax.S...  29.8 us
    pallas_call x1, Pallas kernels, local(): pl.pallas_call(handed_on, out_shape=tuple((jax.ShapeDtypeStruct(x.shape,...  1.54 us

profile of v3, /device:TPU:12, one launch (start us, length us, event | category | flops | bytes accessed | tf_op | source)
XLA Modules:
  0.0 32.0 jit_solution(1981589388977213328)
XLA Ops:
  0.6 29.8 %shard_map.112 = (f32[8,8,256]{2,1,0:T(8,128)}, f32[64,128]{1,0:T(8,128)}, f32[64,128]{1,0:T(8,128)}) custom-call(f32[8,8,256]{2,1,0:T(8,128)} %pressure_hbm.1, f32[8,8,256]{2,1,0:T(8,128)} %previous_hbm.1, f32[64,128]{1,0:T(8,128)} %radius_hbm.1, f32[64,128]{1,0:T(8,128)} %velocity_hbm.1, f32[3,64,128]{2,1,0:T(8,128)} %positions_hbm.1, s32[1,64]{1,0:T(1,128)} %bitcast.2, ...), custom_call_target="tpu_custom_call" | custom-call | tf_op jit(solution)/shard_map/pallas_call | solution.py:503
  30.4 1.5 %shard_map.113 = (f32[8,8,256]{2,1,0:T(8,128)}, f32[64,128]{1,0:T(8,128)}, f32[64,128]{1,0:T(8,128)}) custom-call(f32[8,8,256]{2,1,0:T(8,128)} %get-tuple-element.6.refs_0_, f32[64,128]{1,0:T(8,128)} %get-tuple-element.7.refs_1_, f32[64,128]{1,0:T(8,128)} %get-tuple-element.8.refs_2_), custom_call_target="tpu_custom_call" | custom-call | tf_op jit(solution)/shard_map/pallas_call | solution.py:520

commit v4 on v3

--- a/solution.py
+++ b/solution.py
@@ -35,7 +35,10 @@
     (-1, 0), (1, 0), (0, -1), (0, 1), (-1, -1),
     (1, 0), (0, 1), (1, 1),
     (0, 1), (0, -1), (0, 1), (0, -1), (0, 1),
+    (1, 0), (-1, 0), (0, 1), (0, -1), (1, 1), (-1, -1), (1, -1), (-1, 1),
 )
+MAIL = 13
+MAIL_TILES = (3, 2, 3, 2, 3, 1, 1, 1)
 KINDS = len(OFFSETS)
 
 
@@ -88,6 +91,7 @@
     pressure, previous, radius, velocity, positions, occupancy, anchors, migrations, crossings,
     halo, edge, dep_in, dep_out, fix_in, fix_out, fix, rv_in, rv_out, rv, counts, field,
     rows, placed, fresh, corner_z, take, put, turn, parts, shares, planar, norms, w_high, w_low,
+    mail_in, mail_out, partial, kept,
     send_sem, recv_sem, load_sem,
 ):
     loads = {}
@@ -118,7 +122,7 @@
         return (a >= 0) & (a < slabs) & (b >= 0) & (b < bricks)
 
     barrier = pltpu.get_barrier_semaphore()
-    near = ((1, 0), (-1, 0), (0, 1), (0, -1), (1, 1), (-1, -1))
+    near = OFFSETS[MAIL:]
     expected = jnp.int32(0)
     for dx, dy in near:
         expected = expected + inside(dx, dy).astype(jnp.int32)
@@ -219,16 +223,22 @@
 
         @pl.when(jnp.logical_not(inside(-dx, -dy)))
         def _():
-            for s in range(STEPS):
-                halo[s, kind] = jnp.zeros((cells_y, depth), F32)
+            halo[0, kind] = jnp.zeros((cells_y, depth), F32)
 
     for kind in (DEP_X, DEP_Y, DEP_CORNER):
         dx, dy = OFFSETS[kind]
 
         @pl.when(jnp.logical_not(inside(-dx, -dy)))
         def _():
-            for s in range(STEPS):
-                dep_in[s, kind - 5] = jnp.zeros((cells_y, depth), F32)
+            dep_in[STEPS - 1, kind - 5] = jnp.zeros((cells_y, depth), F32)
+
+    for d in range(8):
+        dx, dy = OFFSETS[MAIL + d]
+
+        @pl.when(jnp.logical_not(inside(-dx, -dy)))
+        def _():
+            for s in range(STEPS - 1):
+                mail_in[s, d] = jnp.zeros((3 * cells_y, depth), F32)
 
     @pl.when(brick == 0)
     def _():
@@ -319,8 +329,9 @@
     for s in range(STEPS):
         now = pressure if s == 0 else field.at[s - 1]
         before = previous if s == 0 else (pressure if s == 1 else field.at[s - 2])
-        for kind in (X_HIGH, Y_HIGH, CORNER):
-            arrive(kind, s, halo.at[s, kind])
+        if s == 0:
+            for kind in range(5):
+                arrive(kind, s, halo.at[s, kind])
         corner_row = jnp.where(iota((cells_y, depth), 0) == 0, halo[s, CORNER], 0.0)
         cells = jnp.concatenate(
             [
@@ -396,9 +407,60 @@
                     placed[at, 128 * part : 128 * (part + 1)] = jnp.where(valid, found, 0.0)
 
         collected = picked(put[s], placed[...], 2)
-        dep_out[s] = collected[own : own + 3 * cells_y, :]
-        for part, kind in enumerate((DEP_X, DEP_Y, DEP_CORNER)):
-            send(kind, s, dep_out.at[s, pl.ds(part * cells_y, cells_y)], dep_in.at[s, part])
+        x_face, y_face, corner_face = [
+            source_gain * collected[own + part * cells_y : own + (part + 1) * cells_y, :]
+            for part in range(3)
+        ]
+        if s + 1 == STEPS:
+            for part, face in enumerate((x_face, y_face, corner_face)):
+                dep_out[s, part * cells_y : (part + 1) * cells_y, :] = face
+            for part, kind in enumerate((DEP_X, DEP_Y, DEP_CORNER)):
+                send(kind, s, dep_out.at[s, pl.ds(part * cells_y, cells_y)], dep_in.at[s, part])
+        after = out_pressure if s + 1 == STEPS else field.at[s]
+        y_at, z_at = iota((cells_y, depth), 0), iota((cells_y, depth), 1)
+        bases = []
+        for x in range(cells_x):
+            here = now[x]
+            around = (halo[s, X_LOW] if x == 0 else now[x - 1]) + (
+                halo[s, X_HIGH] if x == cells_x - 1 else now[x + 1]
+            )
+            around = around + jnp.where(
+                y_at == 0, halo[s, Y_LOW, x : x + 1, :], pltpu.roll(here, 1, 0)
+            )
+            around = around + jnp.where(
+                y_at == cells_y - 1, halo[s, Y_HIGH, x : x + 1, :], pltpu.roll(here, cells_y - 1, 0)
+            )
+            around = around + jnp.where(z_at == 0, 0.0, pltpu.roll(here, 1, 1))
+            around = around + jnp.where(z_at == depth - 1, 0.0, pltpu.roll(here, depth - 1, 1))
+            bases.append(
+                2.0 * here
+                - before[x]
+                + courant_square * (around - 6.0 * here)
+                + source_gain * collected[x * cells_y : (x + 1) * cells_y, :]
+            )
+        if s + 1 < STEPS:
+            y_first = jnp.concatenate([base[0:1, :] for base in bases], axis=0)
+            y_last = jnp.concatenate([base[cells_y - 1 :, :] for base in bases], axis=0)
+            mails = (
+                (x_face, bases[cells_x - 1], corner_face),
+                (bases[0], y_face),
+                (y_face, y_last, corner_face),
+                (y_first, x_face),
+                (corner_face, y_face, x_face),
+                (bases[0],),
+                (x_face,),
+                (y_face,),
+            )
+            for d, mail in enumerate(mails):
+                for part, tile in enumerate(mail):
+                    mail_out[s, d, part * cells_y : (part + 1) * cells_y, :] = tile
+            for d in range(8):
+                size = pl.ds(0, MAIL_TILES[d] * cells_y)
+                send(MAIL + d, s, mail_out.at[s, d, size], mail_in.at[s, d, size])
+        for x in range(cells_x):
+            partial[x] = bases[x]
+        if s + 1 < STEPS:
+            kept[0], kept[1], kept[2] = x_face, y_face, corner_face
         turned = picked(turn[s + 1], fresh[...], 3)
         if s + 1 < STEPS:
             send_rv(s + 1, turned)
@@ -411,39 +473,38 @@
                 send_fix(s + 2, picked(turn[s + 2], fix[s + 1], 3))
             build_weights(s + 1)
 
-        for kind in (X_LOW, Y_LOW):
-            arrive(kind, s, halo.at[s, kind])
-        after = out_pressure if s + 1 == STEPS else field.at[s]
-        y_at, z_at = iota((cells_y, depth), 0), iota((cells_y, depth), 1)
-        bases = []
+        first_row = y_at == 0
+
+        def tile(d, part):
+            return mail_in[s, d, part * cells_y : (part + 1) * cells_y, :]
+
+        if s + 1 == STEPS:
+            for part, kind in enumerate((DEP_X, DEP_Y, DEP_CORNER)):
+                arrive(kind, s, dep_in.at[s, part])
+            at_x, at_y, at_corner = [dep_in[s, part] for part in range(3)]
+        else:
+            for d in range(8):
+                arrive(MAIL + d, s, mail_in.at[s, d, pl.ds(0, MAIL_TILES[d] * cells_y)])
+            at_x, at_y, at_corner = tile(0, 0), tile(2, 0), tile(4, 0)
+
+            def at_first(value):
+                return jnp.where(first_row, value, 0.0)
+
+            last_x = mail_in[s, 4, 2 * cells_y - 1 : 2 * cells_y, :]
+            last_y = mail_in[s, 4, 3 * cells_y - 1 : 3 * cells_y, :]
+            x_high = tile(1, 0) + kept[0] + at_first(tile(2, 2) + tile(7, 0))
+            y_high = tile(3, 0) + kept[1] + at_first(tile(0, 2) + tile(6, 0))
+            corner = tile(5, 0) + kept[2] + tile(1, 1) + tile(3, 1)
+            halo[s + 1, X_HIGH] = jnp.where(inside(1, 0), x_high, 0.0)
+            halo[s + 1, Y_HIGH] = jnp.where(inside(0, 1), y_high, 0.0)
+            halo[s + 1, CORNER] = jnp.where(inside(1, 1), corner, 0.0)
+            halo[s + 1, X_LOW] = tile(0, 1) + at_first(last_x)
+            halo[s + 1, Y_LOW] = tile(2, 1) + at_first(last_y)
         for x in range(cells_x):
-            here = now[x]
-            around = (halo[s, X_LOW] if x == 0 else now[x - 1]) + (
-                halo[s, X_HIGH] if x == cells_x - 1 else now[x + 1]
-            )
-            around = around + jnp.where(
-                y_at == 0, halo[s, Y_LOW, x : x + 1, :], pltpu.roll(here, 1, 0)
-            )
-            around = around + jnp.where(
-                y_at == cells_y - 1, halo[s, Y_HIGH, x : x + 1, :], pltpu.roll(here, cells_y - 1, 0)
-            )
-            around = around + jnp.where(z_at == 0, 0.0, pltpu.roll(here, 1, 1))
-            around = around + jnp.where(z_at == depth - 1, 0.0, pltpu.roll(here, depth - 1, 1))
-            bases.append(
-                2.0 * here
-                - before[x]
-                + courant_square * (around - 6.0 * here)
-                + source_gain * collected[x * cells_y : (x + 1) * cells_y, :]
-            )
-        for part, kind in enumerate((DEP_X, DEP_Y, DEP_CORNER)):
-            arrive(kind, s, dep_in.at[s, part])
-        for x in range(cells_x):
-            extra = jnp.where(y_at == 0, dep_in[s, 1, x : x + 1, :], 0.0)
+            extra = jnp.where(first_row, at_y[x : x + 1, :], 0.0)
             if x == 0:
-                extra = extra + dep_in[s, 0] + dep_in[s, 2]
-            after[x] = bases[x] + source_gain * extra
-        if s + 1 < STEPS:
-            send_halo(s + 1, after)
+                extra = extra + at_x + at_corner
+            after[x] = partial[x] + extra
 
     for there, made in pending:
 
@@ -496,6 +557,10 @@
         pltpu.VMEM((bins, BIN), F32),
         pltpu.VMEM((PZ * bins, BIN), BF16),
         pltpu.VMEM((PZ * bins, BIN), BF16),
+        pltpu.VMEM((STEPS - 1, 8, 3 * cells_y, depth), F32),
+        pltpu.VMEM((STEPS - 1, 8, 3 * cells_y, depth), F32),
+        pltpu.VMEM(pressure.shape, F32),
+        pltpu.VMEM((3, cells_y, depth), F32),
         pltpu.SemaphoreType.DMA((STEPS, KINDS)),
         pltpu.SemaphoreType.DMA((STEPS, KINDS)),
         pltpu.SemaphoreType.DMA((9,)),

time: 32.2 us -> 27.9 us (0.87)
  Pallas kernels: 31.3 us -> 26.9 us
    pallas_call x1, Pallas kernels: 29.8 us -> 25.3 us  [local(): pl.pallas_call(functools.partial(kernel, slabs, bricks), out_shape=(jax.S...]
where the time goes in v4:
time: 27.9 us; the launch traced here: 27.5 us
  Pallas kernels  26.9 us (96%)
  between operations  0.64 us (2%)
    pallas_call x1, Pallas kernels, local(): pl.pallas_call(functools.partial(kernel, slabs, bricks), out_shape=(jax.S...  25.3 us
    pallas_call x1, Pallas kernels, local(): pl.pallas_call(handed_on, out_shape=tuple((jax.ShapeDtypeStruct(x.shape,...  1.54 us

profile of v4, /device:TPU:12, one launch (start us, length us, event | category | flops | bytes accessed | tf_op | source)
XLA Modules:
  0.0 27.5 jit_solution(4630299395245534090)
XLA Ops:
  0.6 25.3 %shard_map.112 = (f32[8,8,256]{2,1,0:T(8,128)}, f32[64,128]{1,0:T(8,128)}, f32[64,128]{1,0:T(8,128)}) custom-call(f32[8,8,256]{2,1,0:T(8,128)} %pressure_hbm.1, f32[8,8,256]{2,1,0:T(8,128)} %previous_hbm.1, f32[64,128]{1,0:T(8,128)} %radius_hbm.1, f32[64,128]{1,0:T(8,128)} %velocity_hbm.1, f32[3,64,128]{2,1,0:T(8,128)} %positions_hbm.1, s32[1,64]{1,0:T(1,128)} %bitcast.2, ...), custom_call_target="tpu_custom_call" | custom-call | tf_op jit(solution)/shard_map/pallas_call | solution.py:568
  26.0 1.5 %shard_map.113 = (f32[8,8,256]{2,1,0:T(8,128)}, f32[64,128]{1,0:T(8,128)}, f32[64,128]{1,0:T(8,128)}) custom-call(f32[8,8,256]{2,1,0:T(8,128)} %get-tuple-element.6.refs_0_, f32[64,128]{1,0:T(8,128)} %get-tuple-element.7.refs_1_, f32[64,128]{1,0:T(8,128)} %get-tuple-element.8.refs_2_), custom_call_target="tpu_custom_call" | custom-call | tf_op jit(solution)/shard_map/pallas_call | solution.py:585

commit v5 on v4

--- a/solution.py
+++ b/solution.py
@@ -278,6 +278,8 @@
     square = iota((patch_rows, patch_rows), 0) == iota((patch_rows, patch_rows), 1)
     for s in range(STEPS):
         turn[s + 1] = turn_of(s + 1)
+
+    def build_corners(s):
         listed_slot = jnp.sum(jnp.where(owner, list_rows[s], 0.0), axis=1, keepdims=True)
         chosen = listed_slot == slot_row
         x, y, z = [
@@ -321,6 +323,7 @@
     fix[0] = merged(FIX_UP, FIX_DOWN, 0, fix_in, fix_out)
     send_fix(1, picked(turn[1], fix[0], 3))
     build_weights(0)
+    build_corners(0)
     loads["previous"].wait()
 
     lane = iota((8, 128), 1)
@@ -472,6 +475,7 @@
             if s + 2 < STEPS:
                 send_fix(s + 2, picked(turn[s + 2], fix[s + 1], 3))
             build_weights(s + 1)
+            build_corners(s + 1)
 
         first_row = y_at == 0
 

time: 27.9 us -> 28.1 us (level)
  no operation moved by 1% of the time
where the time goes in v5:
time: 28.1 us; the launch traced here: 27.8 us
  Pallas kernels  27.1 us (96%)
  between operations  0.64 us (2%)
    pallas_call x1, Pallas kernels, local(): pl.pallas_call(functools.partial(kernel, slabs, bricks), out_shape=(jax.S...  25.6 us
    pallas_call x1, Pallas kernels, local(): pl.pallas_call(handed_on, out_shape=tuple((jax.ShapeDtypeStruct(x.shape,...  1.54 us

profile of v5, /device:TPU:12, one launch (start us, length us, event | category | flops | bytes accessed | tf_op | source)
XLA Modules:
  0.0 27.8 jit_solution(11002743445681511273)
XLA Ops:
  0.6 25.6 %shard_map.112 = (f32[8,8,256]{2,1,0:T(8,128)}, f32[64,128]{1,0:T(8,128)}, f32[64,128]{1,0:T(8,128)}) custom-call(f32[8,8,256]{2,1,0:T(8,128)} %pressure_hbm.1, f32[8,8,256]{2,1,0:T(8,128)} %previous_hbm.1, f32[64,128]{1,0:T(8,128)} %radius_hbm.1, f32[64,128]{1,0:T(8,128)} %velocity_hbm.1, f32[3,64,128]{2,1,0:T(8,128)} %positions_hbm.1, s32[1,64]{1,0:T(1,128)} %bitcast.2, ...), custom_call_target="tpu_custom_call" | custom-call | tf_op jit(solution)/shard_map/pallas_call | solution.py:572
  26.2 1.5 %shard_map.113 = (f32[8,8,256]{2,1,0:T(8,128)}, f32[64,128]{1,0:T(8,128)}, f32[64,128]{1,0:T(8,128)}) custom-call(f32[8,8,256]{2,1,0:T(8,128)} %get-tuple-element.6.refs_0_, f32[64,128]{1,0:T(8,128)} %get-tuple-element.7.refs_1_, f32[64,128]{1,0:T(8,128)} %get-tuple-element.8.refs_2_), custom_call_target="tpu_custom_call" | custom-call | tf_op jit(solution)/shard_map/pallas_call | solution.py:589
